TPU v7x, 32 devices: a whole 2x2x4 slice. The times are simulated.
32 devices in a mesh: lat: 4 (over x, core), lon: 8 (over z, y).
Axes of the slice: x: 2, y: 2, z: 4, core: 2. Of those that a mesh axis runs over, the one named last changes fastest.
Arguments:
- control: float32 [20, 4, 64, 1024], P(None, None, 'lat', 'lon'), may hold values from -6 to 6
- kappa: float32 [64, 1024], P('lat', 'lon'), may hold values from 0.05 to 0.49
- sea_mask: int32 [64, 1024], P('lat', 'lon'), may hold values 0 or 1
- vert_coef: float32 [20, 64, 1024], P(None, 'lat', 'lon'), may hold values from 0.5 to 20
- stencil_offsets: int32 [8, 1024, 1024], P(None, ('lat', 'lon')), may hold values from 0 to 2047
- stencil_weights: float32 [8, 1024, 1024], P(None, ('lat', 'lon')), may hold values from 0.05 to 0.3
- slot_target: int32 [1024, 1024], P(('lat', 'lon')), may hold values from 0 to 8191
- observed: float32 [262144], P(('lat', 'lon')), may hold values from -6 to 6
- inv_error: float32 [262144], P(('lat', 'lon')), may hold values from 0.5 to 2
Outputs:
- increment: float32 [20, 4, 64, 1024], P(None, None, 'lat', 'lon')
- misfit: float32 [262144], P(('lat', 'lon'))
Inputs may be any that keep to these rules, and one draw needn't show every extreme that they name: `stencil_offsets`: an offset indexes one horizontal cell of one device's tile, as row * 128 + column.
All inputs are finite; a program needn't handle non-finite values. No bound on the sum of `sea_mask` on one device may be relied on, other than what follows from the above.
Results may differ from a plain program's by a relative error of at most 0.00002.
Values sent between devices are 32-bit elements; how exact they have to be, the bound alone decides.
A program may use at most 64 MiB of HBM per device.

v0:
```python
import functools

import jax
import jax.numpy as jnp
from jax import lax
from jax.experimental import pallas as pl
from jax.experimental.pallas import tpu as pltpu
from jax.sharding import PartitionSpec as P

STEPS = 10
LANES = 128
SUB = 8


def lane_ids():
    return lax.broadcasted_iota(jnp.int32, (SUB, LANES), 1)


def lay_kernel(rows, layers, field_ref, kappa_ref, mask_ref, out_ref):
    wide = layers + SUB
    coef = kappa_ref[...] * mask_ref[...].astype(jnp.float32)
    for r in range(rows):
        for g in range(layers // SUB):
            out_ref[pl.ds(r * wide + g * SUB, SUB), :] = field_ref[
                pl.ds(g * SUB * rows + r, SUB, stride=rows), :
            ]
        out_ref[pl.ds(r * wide + layers, SUB), :] = jnp.broadcast_to(
            coef[r : r + 1, :], (SUB, LANES)
        )


def pack_kernel(rows, groups, main_ref, north_ref, south_ref, head_ref, tail_ref):
    lane = lane_ids()
    pitch = LANES // groups
    wide = groups * SUB

    def pack(src, count, start):
        def one_row(r, carry):
            base = pl.multiple_of(r * wide, SUB)
            head = jnp.zeros((SUB, LANES), jnp.float32)
            tail = head
            for g in range(groups):
                cells = src[pl.ds(base + g * SUB, SUB), :]
                spot = (lane >= g * pitch) & (lane < g * pitch + STEPS)
                head = jnp.where(spot, pltpu.roll(cells, g * pitch, 1), head)
                move = (g * pitch + STEPS) % LANES
                tail = jnp.where(spot, pltpu.roll(cells, move, 1), tail)
            at = pl.ds(pl.multiple_of((start + r) * SUB, SUB), SUB)
            head_ref[at, :] = head
            tail_ref[at, :] = tail
            return carry

        lax.fori_loop(0, count, one_row, 0, unroll=2)

    pack(north_ref, STEPS, 0)
    pack(main_ref, rows, STEPS)
    pack(south_ref, STEPS, STEPS + rows)


def diffuse(rows, layers, main_ref, north_ref, south_ref, west_ref, east_ref, near, far, near_b, far_b, coefs):
    lane = lane_ids()
    groups = layers // SUB + 1
    pitch = LANES // groups
    wide = groups * SUB
    tall = rows + 2 * STEPS

    def outer(r, g):
        at = pl.ds(pl.multiple_of(r * SUB, SUB), SUB)
        east = pltpu.roll(east_ref[at, :], (LANES - g * pitch) % LANES, 1)
        west = pltpu.roll(west_ref[at, :], (2 * LANES - STEPS - g * pitch) % LANES, 1)
        return jnp.where(lane < STEPS, east, jnp.where(lane >= LANES - STEPS, west, 0.0))

    def fill(src, count, start):
        def one_row(r, carry):
            base = pl.multiple_of(r * wide, SUB)
            row = start + r
            for g in range(groups - 1):
                at = pl.ds(pl.multiple_of(row * layers + g * SUB, SUB), SUB)
                near[at, :] = src[pl.ds(base + g * SUB, SUB), :]
                far[at, :] = outer(row, g)
            at = pl.ds(pl.multiple_of(row * SUB, SUB), SUB)
            coefs[10, at, :] = src[pl.ds(base + layers, SUB), :]
            coefs[11, at, :] = outer(row, groups - 1)
            return carry

        lax.fori_loop(0, count, one_row, 0, unroll=2)

    fill(north_ref, STEPS, 0)
    fill(main_ref, rows, STEPS)
    fill(south_ref, STEPS, STEPS + rows)

    def sides(a, b):
        ra, rb = pltpu.roll(a, 1, 1), pltpu.roll(b, 1, 1)
        la, lb = pltpu.roll(a, LANES - 1, 1), pltpu.roll(b, LANES - 1, 1)
        first, last = lane == 0, lane == LANES - 1
        return (
            (jnp.where(first, rb, ra), jnp.where(last, lb, la)),
            (jnp.where(first, ra, rb), jnp.where(last, la, lb)),
        )

    def weigh(r, carry):
        at = pl.ds(pl.multiple_of(r * SUB, SUB), SUB)
        up = pl.ds(pl.multiple_of((r - 1) * SUB, SUB), SUB)
        down = pl.ds(pl.multiple_of((r + 1) * SUB, SUB), SUB)
        both = sides(coefs[10, at, :], coefs[11, at, :])
        for k in range(2):
            here = coefs[10 + k, at, :]
            n = here * coefs[10 + k, up, :]
            s = here * coefs[10 + k, down, :]
            w = here * both[k][0]
            e = here * both[k][1]
            coefs[5 * k, at, :] = 1.0 - ((n + s) + (w + e))
            coefs[5 * k + 1, at, :] = n
            coefs[5 * k + 2, at, :] = s
            coefs[5 * k + 3, at, :] = w
            coefs[5 * k + 4, at, :] = e
        return carry

    lax.fori_loop(1, tall - 1, weigh, 0, unroll=2)

    for step in range(STEPS):
        old, new = (near, far), (near_b, far_b)
        if step % 2:
            old, new = new, old

        def two_rows(turn, carry, old=old, new=new, first=step + 1):
            r = first + 2 * turn
            c = [
                [coefs[k, pl.ds(pl.multiple_of((r + d) * SUB, SUB), SUB), :] for k in range(10)]
                for d in range(2)
            ]
            for g in range(groups - 1):
                spots = [
                    pl.ds(pl.multiple_of((r + d) * layers + g * SUB, SUB), SUB)
                    for d in range(-1, 3)
                ]
                cells = [[old[k][spot, :] for spot in spots] for k in range(2)]
                results = []
                for d in range(2):
                    both = sides(cells[0][d + 1], cells[1][d + 1])
                    for k in range(2):
                        p = c[d][5 * k : 5 * k + 5]
                        total = p[0] * cells[k][d + 1] + p[1] * cells[k][d]
                        other = p[3] * both[k][0] + p[4] * both[k][1]
                        results.append((k, spots[d + 1], (total + p[2] * cells[k][d + 2]) + other))
                for k, spot, value in results:
                    new[k][spot, :] = value
            return carry

        lax.fori_loop(0, (tall - 2 - 2 * step) // 2, two_rows, 0)


def solve_columns(rows, layers, done, vert_ref, inc_ref):
    levels = vert_ref.shape[0] // rows
    fields = layers // levels
    for h in range(rows // SUB):
        ratio = []
        coef = vert_ref[pl.ds(h * SUB, SUB), :]
        cprev = jnp.zeros((SUB, LANES), jnp.float32)
        prev = [cprev] * fields
        for k in range(levels):
            if k + 1 < levels:
                below = vert_ref[pl.ds((k + 1) * rows + h * SUB, SUB), :]
            else:
                below = jnp.zeros((SUB, LANES), jnp.float32)
            inv = 1.0 / (((1.0 + coef) + below) + coef * cprev)
            cprev = -below * inv
            ratio.append(cprev)
            for f in range(fields):
                layer = k * fields + f
                right = done[pl.ds((STEPS + h * SUB) * layers + layer, SUB, stride=layers), :]
                prev[f] = (right + coef * prev[f]) * inv
                inc_ref[pl.ds(layer * rows + h * SUB, SUB), :] = prev[f]
            coef = below
        for k in range(levels - 2, -1, -1):
            for f in range(fields):
                at = pl.ds((k * fields + f) * rows + h * SUB, SUB)
                prev[f] = inc_ref[at, :] - ratio[k] * prev[f]
                inc_ref[at, :] = prev[f]


def pick(table, row, col):
    level = [jnp.take_along_axis(t, col, axis=1) for t in table]
    bit = 1
    while len(level) > 1:
        odd = (row & bit) != 0
        level = [jnp.where(odd, level[i + 1], level[i]) for i in range(0, len(level), 2)]
        bit *= 2
    return level[0]


def turn_kernel(off_ref, w_ref, off_t, w_t):
    cap = off_ref.shape[1]
    groups = off_ref.shape[0] // LANES
    padded = off_t.shape[1]
    if padded > cap:
        for g in range(groups):
            off_t[g, cap:padded, :] = jnp.zeros((padded - cap, LANES), jnp.int32)
            w_t[g, cap:padded, :] = jnp.zeros((padded - cap, LANES), jnp.float32)
    for g in range(groups):
        for c in range(cap // LANES):
            here = pl.ds(c * LANES, LANES)
            off_t[g, here, :] = off_ref[pl.ds(g * LANES, LANES), here].T
            w_t[g, here, :] = w_ref[pl.ds(g * LANES, LANES), here].T


def column_kernel(
    rows,
    layers,
    owners,
    main_ref,
    north_ref,
    south_ref,
    west_ref,
    east_ref,
    vert_ref,
    off_t,
    w_t,
    inc_ref,
    out_ref,
    near,
    far,
    near_b,
    far_b,
    coefs,
    acc,
):
    diffuse(
        rows, layers, main_ref, north_ref, south_ref, west_ref, east_ref, near, far, near_b, far_b, coefs
    )
    solve_columns(rows, layers, near_b if STEPS % 2 else near, vert_ref, inc_ref)
    cap = out_ref.shape[1]
    groups = off_t.shape[0]
    turns = -(-cap // layers)

    def one_group(lg, carry):
        base = pl.multiple_of(lg * SUB, SUB)
        table = [inc_ref[pl.ds(base * rows + r, SUB, stride=rows), :] for r in range(rows)]
        for m in range(turns):
            at = pl.ds(m * layers + base, SUB)
            total = None
            for g in range(groups):
                idx = off_t[g, at, :]
                term = pick(table, idx >> 7, idx & (LANES - 1)) * w_t[g, at, :]
                total = term if total is None else total + term
            acc[at, :] = total
        return carry

    lax.fori_loop(0, layers // SUB, one_group, 0, unroll=2)
    for c in range(cap // LANES):
        here = pl.ds(c * LANES, LANES)
        block = acc[here, :].T
        total = block[:owners]
        for k in range(1, LANES // owners):
            total = total + block[k * owners : (k + 1) * owners]
        out_ref[:, here] = total


def shift(block, axis, step, closed):
    count = lax.axis_size(axis)
    pairs = [(i, (i + step) % count) for i in range(count)]
    if not closed:
        pairs = [(i, j) for i, j in pairs if j == i + step]
    return lax.ppermute(block, axis, pairs)


def local_call(kernel, shapes, count, scratch=(), name=None):
    return pl.pallas_call(
        kernel,
        out_shape=shapes,
        in_specs=[pl.BlockSpec(memory_space=pltpu.VMEM)] * count,
        out_specs=jax.tree.map(lambda _: pl.BlockSpec(memory_space=pltpu.VMEM), shapes),
        scratch_shapes=list(scratch),
        compiler_params=pltpu.CompilerParams(vmem_limit_bytes=40 * 1024 * 1024),
        name=name,
    )


def floats(*shape):
    return jax.ShapeDtypeStruct(shape, jnp.float32)


def columns_and_partials(control, kappa, sea_mask, vert_coef, offsets, weights):
    levels, fields, rows, cols = control.shape
    layers = levels * fields
    groups = layers // SUB + 1
    wide = groups * SUB
    tall = rows + 2 * STEPS
    sten, owners, cap = offsets.shape
    bundles = sten * owners // LANES
    padded = -(-cap // layers) * layers

    main = local_call(
        functools.partial(lay_kernel, rows, layers), floats(rows * wide, LANES), 3, name="lay"
    )(control.reshape(layers * rows, cols), kappa, sea_mask)
    north = shift(main[(rows - STEPS) * wide :], "lat", 1, False)
    south = shift(main[: STEPS * wide], "lat", -1, False)
    head, tail = local_call(
        functools.partial(pack_kernel, rows, groups),
        (floats(tall * SUB, LANES), floats(tall * SUB, LANES)),
        3,
        name="pack",
    )(main, north, south)
    west = shift(tail, "lon", 1, True)
    east = shift(head, "lon", -1, True)
    off_t, w_t = local_call(
        turn_kernel,
        (
            jax.ShapeDtypeStruct((bundles, padded, LANES), jnp.int32),
            floats(bundles, padded, LANES),
        ),
        2,
        name="turn",
    )(offsets.reshape(sten * owners, cap), weights.reshape(sten * owners, cap))
    increment, partial_value = local_call(
        functools.partial(column_kernel, rows, layers, owners),
        (floats(layers * rows, LANES), floats(owners, cap)),
        8,
        [
            pltpu.VMEM((tall * layers, LANES), jnp.float32),
            pltpu.VMEM((tall * layers, LANES), jnp.float32),
            pltpu.VMEM((tall * layers, LANES), jnp.float32),
            pltpu.VMEM((tall * layers, LANES), jnp.float32),
            pltpu.VMEM((12, tall * SUB, LANES), jnp.float32),
            pltpu.VMEM((padded, LANES), jnp.float32),
        ],
        name="columns",
    )(
        main,
        north,
        south,
        west,
        east,
        vert_coef.reshape(levels * rows, cols),
        off_t,
        w_t,
    )
    return increment.reshape(control.shape), partial_value


def split_parts(v):
    first = v.astype(jnp.bfloat16).astype(jnp.float32)
    rest = v - first
    second = rest.astype(jnp.bfloat16).astype(jnp.float32)
    return first, second, rest - second


def spread(v, t, high):
    cap = v.shape[1]
    hit = lax.broadcasted_iota(jnp.int32, (high, cap), 0) == (t >> 7)
    ones = lax.broadcasted_iota(jnp.int32, (LANES, cap), 0) == (t & (LANES - 1))
    left = jnp.concatenate(
        [jnp.where(hit, part, 0.0).astype(jnp.bfloat16) for part in split_parts(v)], axis=0
    )
    right = jnp.where(ones, 1.0, 0.0).astype(jnp.bfloat16)
    return lax.dot_general(
        left, right, (((1,), (1,)), ((), ())), preferred_element_type=jnp.float32
    )


def scatter_kernel(rec_ref, tgt_ref, obs_ref, err_ref, out_ref, acc):
    high = obs_ref.shape[0]
    acc[...] = jnp.zeros_like(acc)

    def one_source(p, carry):
        acc[...] += spread(rec_ref[pl.ds(p, 1), :], tgt_ref[pl.ds(p, 1), :], high)
        return carry

    lax.fori_loop(0, rec_ref.shape[0], one_source, 0, unroll=8)
    total = acc[:high] + acc[high : 2 * high] + acc[2 * high :]
    out_ref[...] = (total - obs_ref[...]) * err_ref[...]


def scatter_misfit(received, target, observed, inv_error):
    high = observed.shape[0] // LANES
    out = pl.pallas_call(
        scatter_kernel,
        out_shape=jax.ShapeDtypeStruct((high, LANES), jnp.float32),
        in_specs=[pl.BlockSpec(memory_space=pltpu.VMEM)] * 4,
        out_specs=pl.BlockSpec(memory_space=pltpu.VMEM),
        scratch_shapes=[pltpu.VMEM((3 * high, LANES), jnp.float32)],
        compiler_params=pltpu.CompilerParams(vmem_limit_bytes=32 * 1024 * 1024),
        name="scatter_misfit",
    )(received, target, observed.reshape(high, LANES), inv_error.reshape(high, LANES))
    return out.reshape(-1)


def per_device(
    control,
    kappa,
    sea_mask,
    vert_coef,
    stencil_offsets,
    stencil_weights,
    slot_target,
    observed,
    inv_error,
):
    increment, partial_value = columns_and_partials(
        control, kappa, sea_mask, vert_coef, stencil_offsets, stencil_weights
    )
    received = lax.all_to_all(
        partial_value, ("lat", "lon"), split_axis=0, concat_axis=0, tiled=True
    )
    misfit = scatter_misfit(received, slot_target, observed, inv_error)
    return (increment, misfit)


def solution(mesh):
    return jax.shard_map(
        per_device,
        mesh=mesh,
        in_specs=(
            P(None, None, "lat", "lon"),
            P("lat", "lon"),
            P("lat", "lon"),
            P(None, "lat", "lon"),
            P(None, ("lat", "lon"), None),
            P(None, ("lat", "lon"), None),
            P(("lat", "lon"), None),
            P(("lat", "lon")),
            P(("lat", "lon")),
        ),
        out_specs=(P(None, None, "lat", "lon"), P(("lat", "lon"))),
        check_vma=False,
    )
```

profile of v0, /device:TPU:0, one launch (start us, length us, event | category | flops | bytes accessed | tf_op | source)
XLA Modules:
  0.0 75.2 jit_solution(1704971709280305313)
XLA Ops:
  0.6 0.0 copy-start.2
  0.6 1.1 %copy-done.2 = f32[20,4,16,128]{3,2,1,0:T(8,128)S(1)} copy-done((f32[20,4,16,128]{3,2,1,0:T(8,128)S(1)}, f32[20,4,16,128]{3,2,1,0:T(8,128)}, u32[]{:S(2)}) %copy-start.2) | copy-done | bytes 655384
  1.7 0.0 copy-start.7
  1.7 0.7 copy-done.7
  2.4 0.0 copy-start.8
  2.4 0.7 copy-done.8
  3.1 0.2 lay.1.main_ref
  3.3 0.0 copy-start.1
  3.3 0.1 fusion
  3.4 0.0 copy-start
  3.4 1.4 %collective-permute-start.1 = (f32[880,128]{1,0:T(8,128)S(1)}, f32[880,128]{1,0:T(8,128)S(1)}, u32[]{:S(2)}, u32[]{:S(2)}) collective-permute-start(f32[880,128]{1,0:T(8,128)S(1)} %get-tuple-element.14), channel_id=1, source_target_pairs={{8,0},{16,8},{24,16},{9,1},{17,9},{25,17},{10,2},{18,10},{26,18},{... | collective-permute-start | bytes 1351688 | tf_op jit(solution)/shard_map/ppermute | solution.py:264
  4.8 3.1 %collective-permute-start = (f32[880,128]{1,0:T(8,128)S(1)}, f32[880,128]{1,0:T(8,128)S(1)}, u32[]{:S(2)}, u32[]{:S(2)}) collective-permute-start(f32[880,128]{1,0:T(8,128)S(1)} %get-tuple-element.15), channel_id=1, source_target_pairs={{0,8},{8,16},{16,24},{1,9},{9,17},{17,25},{2,10},{10,18},{18,26},{... | collective-permute-start | bytes 1351688 | tf_op jit(solution)/shard_map/ppermute | solution.py:264
  7.9 0.0 collective-permute-done.1.south_ref
  7.9 1.4 %collective-permute-done.north_ref = f32[880,128]{1,0:T(8,128)S(1)} collective-permute-done((f32[880,128]{1,0:T(8,128)S(1)}, f32[880,128]{1,0:T(8,128)S(1)}, u32[]{:S(2)}, u32[]{:S(2)}) %collective-permute-start) | collective-permute-done | bytes 450592 | tf_op jit(solution)/shard_map/ppermute | solution.py:264
  9.3 2.0 %pack.1 = (f32[288,128]{1,0:T(8,128)S(1)}, f32[288,128]{1,0:T(8,128)S(1)}) custom-call(f32[1408,128]{1,0:T(8,128)S(1)} %lay.1.main_ref, f32[880,128]{1,0:T(8,128)S(1)} %collective-permute-done.north_ref, f32[880,128]{1,0:T(8,128)S(1)} %collective-permute-done.1.south_ref), custom_call_target="tpu_custom_call" | custom-call | tf_op jit(solution)/shard_map/pack/pallas_call | solution.py:298
  11.3 0.0 copy-start.3
  11.3 3.0 %collective-permute-start.2 = (f32[288,128]{1,0:T(8,128)S(1)}, f32[288,128]{1,0:T(8,128)S(1)}, u32[]{:S(2)}, u32[]{:S(2)}) collective-permute-start(f32[288,128]{1,0:T(8,128)S(1)} %get-tuple-element.8), channel_id=1, source_target_pairs={{0,1},{1,2},{2,3},{3,4},{4,5},{5,6},{6,7},{7,0},{8,9},{9,10},{10,1... | collective-permute-start | bytes 442376 | tf_op jit(solution)/shard_map/ppermute | solution.py:264
  14.3 3.1 %collective-permute-start.3 = (f32[288,128]{1,0:T(8,128)S(1)}, f32[288,128]{1,0:T(8,128)S(1)}, u32[]{:S(2)}, u32[]{:S(2)}) collective-permute-start(f32[288,128]{1,0:T(8,128)S(1)} %get-tuple-element.9), channel_id=1, source_target_pairs={{0,7},{1,0},{2,1},{3,2},{4,3},{5,4},{6,5},{7,6},{8,15},{9,8},{10,9... | collective-permute-start | bytes 442376 | tf_op jit(solution)/shard_map/ppermute | solution.py:264
  17.4 0.0 copy-done.1
  17.4 0.0 copy-done
  17.4 0.6 turn.1
  18.1 2.6 %collective-permute-done.2.west_ref = f32[288,128]{1,0:T(8,128)S(1)} collective-permute-done((f32[288,128]{1,0:T(8,128)S(1)}, f32[288,128]{1,0:T(8,128)S(1)}, u32[]{:S(2)}, u32[]{:S(2)}) %collective-permute-start.2) | collective-permute-done | bytes 147488 | tf_op jit(solution)/shard_map/ppermute | solution.py:264
  20.6 0.5 collective-permute-done.3.east_ref
  21.1 0.0 copy-done.3
  21.1 0.0 copy-start.4
  21.1 0.0 copy-start.5
  21.1 0.0 copy-start.6
  21.1 30.1 %columns.1 = (f32[1280,128]{1,0:T(8,128)}, f32[32,1024]{1,0:T(8,128)S(1)}) custom-call(f32[1408,128]{1,0:T(8,128)S(1)} %lay.1.main_ref, f32[880,128]{1,0:T(8,128)S(1)} %collective-permute-done.north_ref, f32[880,128]{1,0:T(8,128)S(1)} %collective-permute-done.1.south_ref, f32[288,128]{1,0:T(8,128)S(1)} %collective-permute-done.2.west_ref, ...), custom_call_target="tpu_custom_call" | custom-call | tf_op jit(solution)/shard_map/columns/pallas_call | solution.py:315
  51.2 0.1 copy.11
  51.3 19.0 %all_to_all.11 = f32[32,1,1024]{2,1,0:T(1,128)S(1)} all-to-all(f32[32,1,1024]{2,1,0:T(1,128)S(1)} %copy.11), channel_id=1, replica_groups=mesh['lat'=4,'lon'=8] {'lat','lon'}, dimensions={0} | all-to-all | bytes 262144 | tf_op jit(solution)/shard_map/all_to_all | solution.py:402
  70.4 0.0 copy-done.4
  70.4 0.0 copy-done.5
  70.4 0.0 copy-done.6
  70.4 4.7 %scatter_misfit.1 = f32[64,128]{1,0:T(8,128)} custom-call(f32[32,1024]{1,0:T(8,128)S(1)} %bitcast.15, s32[32,1024]{1,0:T(8,128)S(1)} %copy-done.4, f32[64,128]{1,0:T(8,128)S(1)} %bitcast.18, f32[64,128]{1,0:T(8,128)S(1)} %bitcast.19), custom_call_target="tpu_custom_call" | custom-call | tf_op jit(solution)/shard_map/scatter_misfit/pallas_call | solution.py:376
  (1 shorter events, 0.0 us)
Async XLA Ops:
  0.6 1.1 %copy-start.2 = (f32[20,4,16,128]{3,2,1,0:T(8,128)S(1)}, f32[20,4,16,128]{3,2,1,0:T(8,128)}, u32[]{:S(2)}) copy-start(f32[20,4,16,128]{3,2,1,0:T(8,128)} %param.9) | copy-start | bytes 1966084
  1.7 0.7 copy-start.7
  2.4 0.7 copy-start.8
  3.3 14.1 %copy-start.1 = (f32[8,32,1024]{2,1,0:T(8,128)S(1)}, f32[8,32,1024]{2,1,0:T(8,128)}, u32[]{:S(2)}) copy-start(f32[8,32,1024]{2,1,0:T(8,128)} %param.14) | copy-start | bytes 3145732
  3.4 14.0 %copy-start = (s32[8,32,1024]{2,1,0:T(8,128)S(1)}, s32[8,32,1024]{2,1,0:T(8,128)}, u32[]{:S(2)}) copy-start(s32[8,32,1024]{2,1,0:T(8,128)} %param.13) | copy-start | bytes 3145732
  3.4 4.5 %collective-permute-start.1 = (f32[880,128]{1,0:T(8,128)S(1)}, f32[880,128]{1,0:T(8,128)S(1)}, u32[]{:S(2)}, u32[]{:S(2)}) collective-permute-start(f32[880,128]{1,0:T(8,128)S(1)} %get-tuple-element.14), channel_id=1, source_target_pairs={{8,0},{16,8},{24,16},{9,1},{17,9},{25,17},{10,2},{18,10},{26,18},{... | collective-permute-start | bytes 1351688 | tf_op jit(solution)/shard_map/ppermute | solution.py:264
  4.8 4.5 %collective-permute-start = (f32[880,128]{1,0:T(8,128)S(1)}, f32[880,128]{1,0:T(8,128)S(1)}, u32[]{:S(2)}, u32[]{:S(2)}) collective-permute-start(f32[880,128]{1,0:T(8,128)S(1)} %get-tuple-element.15), channel_id=1, source_target_pairs={{0,8},{8,16},{16,24},{1,9},{9,17},{17,25},{2,10},{10,18},{18,26},{... | collective-permute-start | bytes 1351688 | tf_op jit(solution)/shard_map/ppermute | solution.py:264
  11.3 9.8 %copy-start.3 = (f32[20,16,128]{2,1,0:T(8,128)S(1)}, f32[20,16,128]{2,1,0:T(8,128)}, u32[]{:S(2)}) copy-start(f32[20,16,128]{2,1,0:T(8,128)} %param.12) | copy-start | bytes 491524
  11.3 9.3 %collective-permute-start.2 = (f32[288,128]{1,0:T(8,128)S(1)}, f32[288,128]{1,0:T(8,128)S(1)}, u32[]{:S(2)}, u32[]{:S(2)}) collective-permute-start(f32[288,128]{1,0:T(8,128)S(1)} %get-tuple-element.8), channel_id=1, source_target_pairs={{0,1},{1,2},{2,3},{3,4},{4,5},{5,6},{6,7},{7,0},{8,9},{9,10},{10,1... | collective-permute-start | bytes 442376 | tf_op jit(solution)/shard_map/ppermute | solution.py:264
  14.3 6.7 %collective-permute-start.3 = (f32[288,128]{1,0:T(8,128)S(1)}, f32[288,128]{1,0:T(8,128)S(1)}, u32[]{:S(2)}, u32[]{:S(2)}) collective-permute-start(f32[288,128]{1,0:T(8,128)S(1)} %get-tuple-element.9), channel_id=1, source_target_pairs={{0,7},{1,0},{2,1},{3,2},{4,3},{5,4},{6,5},{7,6},{8,15},{9,8},{10,9... | collective-permute-start | bytes 442376 | tf_op jit(solution)/shard_map/ppermute | solution.py:264
  21.1 49.4 %copy-start.4 = (s32[32,1024]{1,0:T(8,128)S(1)}, s32[32,1024]{1,0:T(8,128)}, u32[]{:S(2)}) copy-start(s32[32,1024]{1,0:T(8,128)} %tgt_ref.1) | copy-start | bytes 393220
  21.1 49.4 %copy-start.5 = (f32[8192]{0:T(1024)S(1)}, f32[8192]{0:T(1024)}, u32[]{:S(2)}) copy-start(f32[8192]{0:T(1024)} %param.16) | copy-start | bytes 98308
  21.1 49.4 %copy-start.6 = (f32[8192]{0:T(1024)S(1)}, f32[8192]{0:T(1024)}, u32[]{:S(2)}) copy-start(f32[8192]{0:T(1024)} %param.17) | copy-start | bytes 98308
where the time goes:
time: 75.5 us; the launch traced here: 75.2 us
  Pallas kernels  37.6 us (50%)
  blocking collectives  19 us (25%)
  starting transfers between devices  10.6 us (14%)
  waiting for transfers between devices  4.38 us (6%)
  local copies, waits for them, and re-layouts  2.72 us (4%)
  between operations  0.76 us (1%)
    pallas_call x1, Pallas kernels, columns_and_partials(): local_call(functools.partial(column_kernel, rows, layers, owners), (float...  30.1 us
    all_to_all x1, blocking collectives, per_device(): lax.all_to_all(partial_value, ('lat', 'lon'), split_axis=0, concat_axis=0...  19 us
    ppermute x4, starting transfers between devices, shift(): return lax.ppermute(block, axis, pairs)  10.6 us
    pallas_call x1, Pallas kernels, scatter_misfit(): pl.pallas_call(scatter_kernel, out_shape=jax.ShapeDtypeStruct((high, LANE...  4.71 us
    ppermute x4, waiting for transfers between devices, shift(): return lax.ppermute(block, axis, pairs)  4.38 us
    unnamed x19, local copies, waits for them, and re-layouts  2.53 us
    pallas_call x1, Pallas kernels, columns_and_partials(): local_call(functools.partial(pack_kernel, rows, groups), (floats(tall * S...  1.99 us
  transfers between devices with their start and end apart: 4, of which 3 were waited for; matrix products, arithmetic and copies ran while one was open for 0% of the time, Pallas kernels for 1%

commit v1 on v0

--- a/solution.py
+++ b/solution.py
@@ -229,7 +229,8 @@
         rows, layers, main_ref, north_ref, south_ref, west_ref, east_ref, near, far, near_b, far_b, coefs
     )
     solve_columns(rows, layers, near_b if STEPS % 2 else near, vert_ref, inc_ref)
-    cap = out_ref.shape[1]
+    blocks = out_ref.shape[0] // owners
+    cap = blocks * LANES
     groups = off_t.shape[0]
     turns = -(-cap // layers)
 
@@ -253,7 +254,7 @@
         total = block[:owners]
         for k in range(1, LANES // owners):
             total = total + block[k * owners : (k + 1) * owners]
-        out_ref[:, here] = total
+        out_ref[pl.ds(c, owners, stride=blocks), :] = total
 
 
 def shift(block, axis, step, closed):
@@ -314,7 +315,7 @@
     )(offsets.reshape(sten * owners, cap), weights.reshape(sten * owners, cap))
     increment, partial_value = local_call(
         functools.partial(column_kernel, rows, layers, owners),
-        (floats(layers * rows, LANES), floats(owners, cap)),
+        (floats(layers * rows, LANES), floats(owners * cap // LANES, LANES)),
         8,
         [
             pltpu.VMEM((tall * layers, LANES), jnp.float32),
@@ -335,22 +336,16 @@
         off_t,
         w_t,
     )
-    return increment.reshape(control.shape), partial_value
-
-
-def split_parts(v):
-    first = v.astype(jnp.bfloat16).astype(jnp.float32)
-    rest = v - first
-    second = rest.astype(jnp.bfloat16).astype(jnp.float32)
-    return first, second, rest - second
+    return increment.reshape(control.shape), partial_value.reshape(owners, cap // LANES, LANES)
 
 
 def spread(v, t, high):
     cap = v.shape[1]
     hit = lax.broadcasted_iota(jnp.int32, (high, cap), 0) == (t >> 7)
     ones = lax.broadcasted_iota(jnp.int32, (LANES, cap), 0) == (t & (LANES - 1))
+    first = v.astype(jnp.bfloat16).astype(jnp.float32)
     left = jnp.concatenate(
-        [jnp.where(hit, part, 0.0).astype(jnp.bfloat16) for part in split_parts(v)], axis=0
+        [jnp.where(hit, part, 0.0).astype(jnp.bfloat16) for part in (first, v - first)], axis=0
     )
     right = jnp.where(ones, 1.0, 0.0).astype(jnp.bfloat16)
     return lax.dot_general(
@@ -358,30 +353,87 @@
     )
 
 
-def scatter_kernel(rec_ref, tgt_ref, obs_ref, err_ref, out_ref, acc):
+def owner_kernel(n_lon, devices, part_ref, tgt_ref, obs_ref, err_ref, out_ref, recv, acc, send_sem, recv_sem):
     high = obs_ref.shape[0]
+    blocks = part_ref.shape[1]
+    me = lax.axis_index("lat") * n_lon + lax.axis_index("lon")
+
+    def place(q):
+        return (q // n_lon, q % n_lon)
+
+    def copy(k):
+        q = lax.rem(me + k, devices)
+        return pltpu.make_async_remote_copy(
+            src_ref=part_ref.at[q],
+            dst_ref=recv.at[k],
+            send_sem=send_sem.at[k],
+            recv_sem=recv_sem.at[k],
+            device_id=place(q),
+            device_id_type=pl.DeviceIdType.MESH,
+        )
+
+    barrier = pltpu.get_barrier_semaphore()
+
+    def greet(k, carry):
+        q = lax.rem(me + k, devices)
+        pl.semaphore_signal(
+            barrier, inc=1, device_id=place(q), device_id_type=pl.DeviceIdType.MESH
+        )
+        return carry
+
+    lax.fori_loop(1, devices, greet, 0)
+    recv[0] = part_ref[me]
     acc[...] = jnp.zeros_like(acc)
-
-    def one_source(p, carry):
-        acc[...] += spread(rec_ref[pl.ds(p, 1), :], tgt_ref[pl.ds(p, 1), :], high)
-        return carry
-
-    lax.fori_loop(0, rec_ref.shape[0], one_source, 0, unroll=8)
-    total = acc[:high] + acc[high : 2 * high] + acc[2 * high :]
-    out_ref[...] = (total - obs_ref[...]) * err_ref[...]
-
-
-def scatter_misfit(received, target, observed, inv_error):
+    pl.semaphore_wait(barrier, devices - 1)
+
+    def send(k, carry):
+        copy(k).start()
+        return carry
+
+    lax.fori_loop(1, devices, send, 0)
+
+    def add(k):
+        p = lax.rem(me - k + devices, devices)
+        cells = recv[k]
+        v = jnp.concatenate([cells[c : c + 1, :] for c in range(blocks)], axis=1)
+        acc[...] += spread(v, tgt_ref[pl.ds(p, 1), :], high)
+
+    add(0)
+
+    def one_source(k, carry):
+        copy(k).wait_recv()
+        add(k)
+        return carry
+
+    lax.fori_loop(1, devices, one_source, 0)
+
+    def drain(k, carry):
+        copy(k).wait_send()
+        return carry
+
+    lax.fori_loop(1, devices, drain, 0)
+    out_ref[...] = (acc[:high] + acc[high:] - obs_ref[...]) * err_ref[...]
+
+
+def owner_misfit(partial_value, target, observed, inv_error):
     high = observed.shape[0] // LANES
+    devices, blocks, _ = partial_value.shape
     out = pl.pallas_call(
-        scatter_kernel,
+        functools.partial(owner_kernel, lax.axis_size("lon"), devices),
         out_shape=jax.ShapeDtypeStruct((high, LANES), jnp.float32),
         in_specs=[pl.BlockSpec(memory_space=pltpu.VMEM)] * 4,
         out_specs=pl.BlockSpec(memory_space=pltpu.VMEM),
-        scratch_shapes=[pltpu.VMEM((3 * high, LANES), jnp.float32)],
-        compiler_params=pltpu.CompilerParams(vmem_limit_bytes=32 * 1024 * 1024),
-        name="scatter_misfit",
-    )(received, target, observed.reshape(high, LANES), inv_error.reshape(high, LANES))
+        scratch_shapes=[
+            pltpu.VMEM(partial_value.shape, jnp.float32),
+            pltpu.VMEM((2 * high, LANES), jnp.float32),
+            pltpu.SemaphoreType.DMA((devices,)),
+            pltpu.SemaphoreType.DMA((devices,)),
+        ],
+        compiler_params=pltpu.CompilerParams(
+            vmem_limit_bytes=32 * 1024 * 1024, collective_id=1, has_side_effects=True
+        ),
+        name="owner_misfit",
+    )(partial_value, target, observed.reshape(high, LANES), inv_error.reshape(high, LANES))
     return out.reshape(-1)
 
 
@@ -399,10 +451,7 @@
     increment, partial_value = columns_and_partials(
         control, kappa, sea_mask, vert_coef, stencil_offsets, stencil_weights
     )
-    received = lax.all_to_all(
-        partial_value, ("lat", "lon"), split_axis=0, concat_axis=0, tiled=True
-    )
-    misfit = scatter_misfit(received, slot_target, observed, inv_error)
+    misfit = owner_misfit(partial_value, slot_target, observed, inv_error)
     return (increment, misfit)
 
 

time: 75.5 us -> 74.1 us (0.981)
  blocking collectives: 19 us -> 0 us
  Pallas kernels: 37.6 us -> 54.8 us
    all_to_all x1 -> x0, blocking collectives: 19 us -> none  [per_device(): lax.all_to_all(partial_value, ('lat', 'lon'), split_axis=0, concat_axis=0...]
    pallas_call x1, Pallas kernels: 4.71 us -> 21.8 us  [owner_misfit(): pl.pallas_call(functools.partial(owner_kernel, lax.axis_size('lon'), devi...]
where the time goes in v1:
time: 74.1 us; the launch traced here: 73.7 us
  Pallas kernels  54.8 us (74%)
  starting transfers between devices  10.6 us (14%)
  waiting for transfers between devices  4.38 us (6%)
  local copies, waits for them, and re-layouts  3.18 us (4%)
    pallas_call x1, Pallas kernels, columns_and_partials(): local_call(functools.partial(column_kernel, rows, layers, owners), (float...  30.1 us
    pallas_call x1, Pallas kernels, owner_misfit(): pl.pallas_call(functools.partial(owner_kernel, lax.axis_size('lon'), devi...  21.8 us
    ppermute x4, starting transfers between devices, shift(): return lax.ppermute(block, axis, pairs)  10.6 us
    ppermute x4, waiting for transfers between devices, shift(): return lax.ppermute(block, axis, pairs)  4.38 us
    unnamed x19, local copies, waits for them, and re-layouts  3.12 us
    pallas_call x1, Pallas kernels, columns_and_partials(): local_call(functools.partial(pack_kernel, rows, groups), (floats(tall * S...  1.99 us
  transfers between devices with their start and end apart: 4, of which 3 were waited for; matrix products, arithmetic and copies ran while one was open for 0% of the time, Pallas kernels for 1%

profile of v1, /device:TPU:0, one launch (start us, length us, event | category | flops | bytes accessed | tf_op | source)
XLA Modules:
  0.0 73.7 jit_solution(7547593865057307136)
XLA Ops:
  0.6 0.0 copy-start.2
  0.6 1.1 %copy-done.2 = f32[20,4,16,128]{3,2,1,0:T(8,128)S(1)} copy-done((f32[20,4,16,128]{3,2,1,0:T(8,128)S(1)}, f32[20,4,16,128]{3,2,1,0:T(8,128)}, u32[]{:S(2)}) %copy-start.2) | copy-done | bytes 655384
  1.7 0.0 copy-start.7
  1.7 0.7 copy-done.7
  2.4 0.0 copy-start.8
  2.4 0.7 copy-done.8
  3.1 0.2 lay.1.main_ref
  3.3 0.0 copy-start.1
  3.3 0.1 fusion
  3.4 0.0 copy-start
  3.4 1.4 %collective-permute-start.1 = (f32[880,128]{1,0:T(8,128)S(1)}, f32[880,128]{1,0:T(8,128)S(1)}, u32[]{:S(2)}, u32[]{:S(2)}) collective-permute-start(f32[880,128]{1,0:T(8,128)S(1)} %get-tuple-element.14), channel_id=1, source_target_pairs={{8,0},{16,8},{24,16},{9,1},{17,9},{25,17},{10,2},{18,10},{26,18},{... | collective-permute-start | bytes 1351688 | tf_op jit(solution)/shard_map/ppermute | solution.py:265
  4.8 3.1 %collective-permute-start = (f32[880,128]{1,0:T(8,128)S(1)}, f32[880,128]{1,0:T(8,128)S(1)}, u32[]{:S(2)}, u32[]{:S(2)}) collective-permute-start(f32[880,128]{1,0:T(8,128)S(1)} %get-tuple-element.15), channel_id=1, source_target_pairs={{0,8},{8,16},{16,24},{1,9},{9,17},{17,25},{2,10},{10,18},{18,26},{... | collective-permute-start | bytes 1351688 | tf_op jit(solution)/shard_map/ppermute | solution.py:265
  7.9 0.0 collective-permute-done.1.south_ref
  7.9 1.4 %collective-permute-done.north_ref = f32[880,128]{1,0:T(8,128)S(1)} collective-permute-done((f32[880,128]{1,0:T(8,128)S(1)}, f32[880,128]{1,0:T(8,128)S(1)}, u32[]{:S(2)}, u32[]{:S(2)}) %collective-permute-start) | collective-permute-done | bytes 450592 | tf_op jit(solution)/shard_map/ppermute | solution.py:265
  9.3 2.0 %pack.1 = (f32[288,128]{1,0:T(8,128)S(1)}, f32[288,128]{1,0:T(8,128)S(1)}) custom-call(f32[1408,128]{1,0:T(8,128)S(1)} %lay.1.main_ref, f32[880,128]{1,0:T(8,128)S(1)} %collective-permute-done.north_ref, f32[880,128]{1,0:T(8,128)S(1)} %collective-permute-done.1.south_ref), custom_call_target="tpu_custom_call" | custom-call | tf_op jit(solution)/shard_map/pack/pallas_call | solution.py:299
  11.3 0.0 copy-start.3
  11.3 3.0 %collective-permute-start.2 = (f32[288,128]{1,0:T(8,128)S(1)}, f32[288,128]{1,0:T(8,128)S(1)}, u32[]{:S(2)}, u32[]{:S(2)}) collective-permute-start(f32[288,128]{1,0:T(8,128)S(1)} %get-tuple-element.8), channel_id=1, source_target_pairs={{0,1},{1,2},{2,3},{3,4},{4,5},{5,6},{6,7},{7,0},{8,9},{9,10},{10,1... | collective-permute-start | bytes 442376 | tf_op jit(solution)/shard_map/ppermute | solution.py:265
  14.3 3.1 %collective-permute-start.3 = (f32[288,128]{1,0:T(8,128)S(1)}, f32[288,128]{1,0:T(8,128)S(1)}, u32[]{:S(2)}, u32[]{:S(2)}) collective-permute-start(f32[288,128]{1,0:T(8,128)S(1)} %get-tuple-element.9), channel_id=1, source_target_pairs={{0,7},{1,0},{2,1},{3,2},{4,3},{5,4},{6,5},{7,6},{8,15},{9,8},{10,9... | collective-permute-start | bytes 442376 | tf_op jit(solution)/shard_map/ppermute | solution.py:265
  17.4 0.0 copy-done.1
  17.4 0.0 copy-done
  17.4 0.6 turn.1
  18.1 2.6 %collective-permute-done.2.west_ref = f32[288,128]{1,0:T(8,128)S(1)} collective-permute-done((f32[288,128]{1,0:T(8,128)S(1)}, f32[288,128]{1,0:T(8,128)S(1)}, u32[]{:S(2)}, u32[]{:S(2)}) %collective-permute-start.2) | collective-permute-done | bytes 147488 | tf_op jit(solution)/shard_map/ppermute | solution.py:265
  20.6 0.5 collective-permute-done.3.east_ref
  21.1 0.0 copy-done.3
  21.1 0.0 copy-start.4
  21.1 0.0 copy-start.5
  21.1 0.0 copy-start.6
  21.1 30.1 %columns.1 = (f32[1280,128]{1,0:T(8,128)}, f32[256,128]{1,0:T(8,128)S(1)}) custom-call(f32[1408,128]{1,0:T(8,128)S(1)} %lay.1.main_ref, f32[880,128]{1,0:T(8,128)S(1)} %collective-permute-done.north_ref, f32[880,128]{1,0:T(8,128)S(1)} %collective-permute-done.1.south_ref, f32[288,128]{1,0:T(8,128)S(1)} %collective-permute-done.2.west_ref, ...), custom_call_target="tpu_custom_call" | custom-call | tf_op jit(solution)/shard_map/columns/pallas_call | solution.py:316
  51.2 0.0 copy-done.4
  51.2 0.0 copy-done.5
  51.2 0.0 copy-done.6
  51.2 21.8 %owner_misfit.1 = f32[64,128]{1,0:T(8,128)S(1)} custom-call(f32[32,8,128]{2,1,0:T(8,128)S(1)} %bitcast.13, s32[32,1024]{1,0:T(8,128)S(1)} %copy-done.4, f32[64,128]{1,0:T(8,128)S(1)} %bitcast.15, f32[64,128]{1,0:T(8,128)S(1)} %bitcast.16), custom_call_target="tpu_custom_call" | custom-call | tf_op jit(solution)/shard_map/owner_misfit/pallas_call | solution.py:421
  73.1 0.6 copy.12
Async XLA Ops:
  0.6 1.1 %copy-start.2 = (f32[20,4,16,128]{3,2,1,0:T(8,128)S(1)}, f32[20,4,16,128]{3,2,1,0:T(8,128)}, u32[]{:S(2)}) copy-start(f32[20,4,16,128]{3,2,1,0:T(8,128)} %param.9) | copy-start | bytes 1966084
  1.7 0.7 copy-start.7
  2.4 0.7 copy-start.8
  3.3 14.1 %copy-start.1 = (f32[8,32,1024]{2,1,0:T(8,128)S(1)}, f32[8,32,1024]{2,1,0:T(8,128)}, u32[]{:S(2)}) copy-start(f32[8,32,1024]{2,1,0:T(8,128)} %param.14) | copy-start | bytes 3145732
  3.4 14.0 %copy-start = (s32[8,32,1024]{2,1,0:T(8,128)S(1)}, s32[8,32,1024]{2,1,0:T(8,128)}, u32[]{:S(2)}) copy-start(s32[8,32,1024]{2,1,0:T(8,128)} %param.13) | copy-start | bytes 3145732
  3.4 4.5 %collective-permute-start.1 = (f32[880,128]{1,0:T(8,128)S(1)}, f32[880,128]{1,0:T(8,128)S(1)}, u32[]{:S(2)}, u32[]{:S(2)}) collective-permute-start(f32[880,128]{1,0:T(8,128)S(1)} %get-tuple-element.14), channel_id=1, source_target_pairs={{8,0},{16,8},{24,16},{9,1},{17,9},{25,17},{10,2},{18,10},{26,18},{... | collective-permute-start | bytes 1351688 | tf_op jit(solution)/shard_map/ppermute | solution.py:265
  4.8 4.5 %collective-permute-start = (f32[880,128]{1,0:T(8,128)S(1)}, f32[880,128]{1,0:T(8,128)S(1)}, u32[]{:S(2)}, u32[]{:S(2)}) collective-permute-start(f32[880,128]{1,0:T(8,128)S(1)} %get-tuple-element.15), channel_id=1, source_target_pairs={{0,8},{8,16},{16,24},{1,9},{9,17},{17,25},{2,10},{10,18},{18,26},{... | collective-permute-start | bytes 1351688 | tf_op jit(solution)/shard_map/ppermute | solution.py:265
  11.3 9.8 %copy-start.3 = (f32[20,16,128]{2,1,0:T(8,128)S(1)}, f32[20,16,128]{2,1,0:T(8,128)}, u32[]{:S(2)}) copy-start(f32[20,16,128]{2,1,0:T(8,128)} %param.12) | copy-start | bytes 491524
  11.3 9.3 %collective-permute-start.2 = (f32[288,128]{1,0:T(8,128)S(1)}, f32[288,128]{1,0:T(8,128)S(1)}, u32[]{:S(2)}, u32[]{:S(2)}) collective-permute-start(f32[288,128]{1,0:T(8,128)S(1)} %get-tuple-element.8), channel_id=1, source_target_pairs={{0,1},{1,2},{2,3},{3,4},{4,5},{5,6},{6,7},{7,0},{8,9},{9,10},{10,1... | collective-permute-start | bytes 442376 | tf_op jit(solution)/shard_map/ppermute | solution.py:265
  14.3 6.7 %collective-permute-start.3 = (f32[288,128]{1,0:T(8,128)S(1)}, f32[288,128]{1,0:T(8,128)S(1)}, u32[]{:S(2)}, u32[]{:S(2)}) collective-permute-start(f32[288,128]{1,0:T(8,128)S(1)} %get-tuple-element.9), channel_id=1, source_target_pairs={{0,7},{1,0},{2,1},{3,2},{4,3},{5,4},{6,5},{7,6},{8,15},{9,8},{10,9... | collective-permute-start | bytes 442376 | tf_op jit(solution)/shard_map/ppermute | solution.py:265
  21.1 30.1 %copy-start.4 = (s32[32,1024]{1,0:T(8,128)S(1)}, s32[32,1024]{1,0:T(8,128)}, u32[]{:S(2)}) copy-start(s32[32,1024]{1,0:T(8,128)} %tgt_ref.1) | copy-start | bytes 393220
  21.1 30.1 %copy-start.5 = (f32[8192]{0:T(1024)S(1)}, f32[8192]{0:T(1024)}, u32[]{:S(2)}) copy-start(f32[8192]{0:T(1024)} %param.16) | copy-start | bytes 98308
  21.1 30.1 %copy-start.6 = (f32[8192]{0:T(1024)S(1)}, f32[8192]{0:T(1024)}, u32[]{:S(2)}) copy-start(f32[8192]{0:T(1024)} %param.17) | copy-start | bytes 98308

commit v2 on v1

v2 whole, which is shorter than its diff:
```python
import functools

import jax
import jax.numpy as jnp
from jax import lax
from jax.experimental import pallas as pl
from jax.experimental.pallas import tpu as pltpu
from jax.sharding import PartitionSpec as P

STEPS = 10
LANES = 128
SUB = 8


WAYS = ((-1, 0), (1, 0), (0, -1), (0, 1), (-1, -1), (-1, 1), (1, -1), (1, 1))
PAD = 16
PITCH = LANES + 2 * PAD


def aligned(start, size):
    return pl.ds(pl.multiple_of(start, SUB), size)


def corner_spots():
    spots, at = [], 0
    for d in range(1, STEPS):
        spots.append((d, at, STEPS - d))
        at += STEPS - d
    return spots, -(-at // SUB) * SUB


def update(old, new, c0, k2, count, first, low, high):
    def two_rows(turn, carry):
        base = (first + 2 * turn) * PITCH
        for v in range(low, high):
            spot = [aligned(base + d * PITCH + v * SUB, SUB) for d in range(-1, 3)]
            cells = [old[s, :] for s in spot]
            for d in range(2):
                at = base + d * PITCH + v * SUB
                side = old[pl.ds(at - 1, SUB), :] + old[pl.ds(at + 1, SUB), :]
                around = (cells[d] + cells[d + 2]) + side
                new[spot[d + 1], :] = c0[spot[d + 1], :] * cells[d + 1] + k2[spot[d + 1], :] * around
        return carry

    lax.fori_loop(0, count, two_rows, 0)


def diffuse(rows, old, new, c0, k2):
    tall = rows + 2 * STEPS
    width = PITCH // SUB
    update(old, new, c0, k2, (tall - 2) // 2, 1, 0, width)
    update(new, old, c0, k2, (tall - 4) // 2, 2, 1, width - 1)

    def two_steps(s, carry):
        first = 2 * s + 1
        update(old, new, c0, k2, (tall - 2 * first) // 2, first, 1, width - 1)
        update(new, old, c0, k2, (tall - 2 * first - 2) // 2, first + 1, 1, width - 1)
        return carry

    lax.fori_loop(1, STEPS // 2, two_steps, 0)


def solve_columns(rows, layers, done, control, coef, vert_ref, inc_ref):
    levels = vert_ref.shape[0] // rows
    fields = layers // levels
    for h in range(rows // SUB):
        here = coef[pl.ds(rows + h * SUB, SUB), :]
        sea = here != 0.0
        back = 1.0 / jnp.where(sea, here, 1.0)
        ratio = []
        above = vert_ref[pl.ds(h * SUB, SUB), :]
        cprev = jnp.zeros((SUB, LANES), jnp.float32)
        prev = [cprev] * fields
        for k in range(levels):
            if k + 1 < levels:
                below = vert_ref[pl.ds((k + 1) * rows + h * SUB, SUB), :]
            else:
                below = jnp.zeros((SUB, LANES), jnp.float32)
            inv = 1.0 / (((1.0 + above) + below) + above * cprev)
            cprev = -below * inv
            ratio.append(cprev)
            for f in range(fields):
                layer = k * fields + f
                at = pl.ds(layer * rows + h * SUB, SUB)
                right = done[pl.ds(h * SUB * LANES + layer, SUB, stride=LANES), :] * back
                right = jnp.where(sea, right, control[at, :])
                prev[f] = (right + above * prev[f]) * inv
                inc_ref[at, :] = prev[f]
            above = below
        for k in range(levels - 2, -1, -1):
            for f in range(fields):
                at = pl.ds((k * fields + f) * rows + h * SUB, SUB)
                prev[f] = inc_ref[at, :] - ratio[k] * prev[f]
                inc_ref[at, :] = prev[f]


def weigh(rows, coefs, held):
    lane = lax.broadcasted_iota(jnp.int32, (40, LANES), 1)
    mid = pl.ds(rows - STEPS + 1, 40)
    up = pl.ds(rows - STEPS, 40)
    down = pl.ds(rows - STEPS + 2, 40)
    here = [coefs[k, mid, :] for k in range(3)]
    right = [pltpu.roll(c, 1, 1) for c in here]
    left = [pltpu.roll(c, LANES - 1, 1) for c in here]
    first, last = lane == 0, lane == LANES - 1
    wests = [right[0], jnp.where(first, right[0], right[1]), jnp.where(first, right[1], right[2])]
    easts = [jnp.where(last, left[1], left[0]), jnp.where(last, left[2], left[1]), left[2]]
    for k in range(3):
        around = (coefs[k, up, :] + coefs[k, down, :]) + (wests[k] + easts[k])
        held[0, k, :, :] = 1.0 - here[k] * around
        held[1, k, :, :] = here[k] * here[k]


def broaden(rows, held, kind, out):
    lane = lax.broadcasted_iota(jnp.int32, (40, LANES), 1)
    rest = jnp.zeros((LANES - 40, LANES), jnp.float32)
    main = jnp.concatenate([held[kind, 1, :, :], rest], axis=0).T
    outer = jnp.where(lane >= LANES - PAD, held[kind, 0, :, :], held[kind, 2, :, :])
    outer = jnp.concatenate([outer, rest], axis=0).T
    for j in range(rows + 2 * STEPS - 2):
        base = (j + 1) * PITCH
        column = outer[:, j : j + 1]
        out[pl.ds(base, PAD), :] = jnp.broadcast_to(column[LANES - PAD :], (PAD, LANES))
        out[pl.ds(base + PAD, LANES), :] = jnp.broadcast_to(main[:, j : j + 1], (LANES, LANES))
        out[pl.ds(base + PAD + LANES, PAD), :] = jnp.broadcast_to(column[:PAD], (PAD, LANES))


def turn(off_ref, w_ref, off_t, w_t):
    cap = off_ref.shape[1]
    groups = off_ref.shape[0] // LANES
    padded = off_t.shape[1]
    if padded > cap:
        for g in range(groups):
            off_t[g, cap:padded, :] = jnp.zeros((padded - cap, LANES), jnp.int32)
            w_t[g, cap:padded, :] = jnp.zeros((padded - cap, LANES), jnp.float32)
    for g in range(groups):
        for c in range(cap // LANES):
            here = pl.ds(c * LANES, LANES)
            off_t[g, here, :] = off_ref[pl.ds(g * LANES, LANES), here].T
            w_t[g, here, :] = w_ref[pl.ds(g * LANES, LANES), here].T


def field_kernel(
    n_lat,
    n_lon,
    rows,
    layers,
    control_ref,
    kappa_ref,
    mask_ref,
    vert_ref,
    off_ref,
    w_ref,
    inc_ref,
    off_t,
    w_t,
    control,
    kappa,
    mask,
    vert,
    off,
    weight,
    coefs,
    held,
    laid,
    far_rows,
    side_out,
    side_in,
    corner_out,
    corner_in,
    near,
    far,
    c0,
    k2,
    done,
    load_sem,
    coef_send,
    coef_recv,
    send_sem,
    recv_sem,
):
    lat, lon = lax.axis_index("lat"), lax.axis_index("lon")
    tall = rows + 2 * STEPS
    pairs = ((control_ref, control), (kappa_ref, kappa), (mask_ref, mask))
    pairs += ((vert_ref, vert), (off_ref, off), (w_ref, weight))
    loads = [pltpu.make_async_copy(a, b, load_sem.at[i]) for i, (a, b) in enumerate(pairs)]
    for i in (1, 2, 0, 3, 4, 5):
        loads[i].start()

    def place(i):
        return (lat + WAYS[i][0], lax.rem(lon + WAYS[i][1] + n_lon, n_lon))

    def guard(step, body):
        if step == 0:
            body()
        else:
            pl.when(lat > 0 if step < 0 else lat < n_lat - 1)(body)

    side_in[...] = jnp.zeros_like(side_in)
    corner_in[...] = jnp.zeros_like(corner_in)

    @pl.when(lat == 0)
    def _():
        coefs[:, :rows, :] = jnp.zeros((3, rows, LANES), jnp.float32)
        far_rows[1] = jnp.zeros((STEPS * layers, LANES), jnp.float32)

    @pl.when(lat == n_lat - 1)
    def _():
        coefs[:, 2 * rows :, :] = jnp.zeros((3, rows, LANES), jnp.float32)
        far_rows[0] = jnp.zeros((STEPS * layers, LANES), jnp.float32)

    barrier = pltpu.get_barrier_semaphore()
    for i, way in enumerate(WAYS):
        guard(
            way[0],
            lambda i=i: pl.semaphore_signal(
                barrier, inc=1, device_id=place(i), device_id_type=pl.DeviceIdType.MESH
            ),
        )

    def remote(i, src, dst, out_sem, in_sem):
        return pltpu.make_async_remote_copy(
            src_ref=src,
            dst_ref=dst,
            send_sem=out_sem.at[i],
            recv_sem=in_sem.at[i],
            device_id=place(i),
            device_id_type=pl.DeviceIdType.MESH,
        )

    def coef_copy(i):
        dl, dn = WAYS[i]
        return remote(
            i, coefs.at[1, pl.ds(rows, rows)], coefs.at[1 - dn, pl.ds((1 - dl) * rows, rows)], coef_send, coef_recv
        )

    spots, corner_size = corner_spots()

    def field_copy(i):
        dl, dn = WAYS[i]
        if dn == 0:
            start = 0 if dl < 0 else (rows - STEPS) * layers
            src = laid.at[pl.ds(start, STEPS * layers)]
            dst = far_rows.at[i]
        elif dl == 0:
            src = side_out.at[i - 2, pl.ds(0, rows * STEPS)]
            dst = side_in.at[i - 2, pl.ds(PAD, rows * STEPS)]
        else:
            src = corner_out.at[i - 4, pl.ds(0, corner_size)]
            dst = corner_in.at[i - 4, pl.ds(PAD, corner_size)]
        return remote(i, src, dst, send_sem, recv_sem)

    loads[1].wait()
    loads[2].wait()
    coefs[1, pl.ds(rows, rows), :] = kappa[...] * mask[...].astype(jnp.float32)
    north, south = (lat > 0).astype(jnp.int32), (lat < n_lat - 1).astype(jnp.int32)
    pl.semaphore_wait(barrier, 2 + 3 * (north + south))
    for i, way in enumerate(WAYS):
        guard(way[0], lambda i=i: coef_copy(i).start())

    loads[0].wait()
    for r in range(rows):
        here = coefs[1, pl.ds(rows + r, 1), :]
        for g in range(layers // SUB):
            laid[pl.ds(r * layers + g * SUB, SUB), :] = (
                control[pl.ds(g * SUB * rows + r, SUB, stride=rows), :] * here
            )
    guard(-1, lambda: field_copy(0).start())
    guard(1, lambda: field_copy(1).start())

    def upright(block):
        return jnp.concatenate([block, block[: LANES - layers]], axis=0).T

    def main_row(r, carry):
        block = laid[aligned(r * layers, layers), :]
        near[aligned((r + STEPS) * PITCH + PAD, LANES), :] = upright(block)
        return carry

    lax.fori_loop(0, rows, main_row, 0, unroll=2)
    for k, first in ((0, PAD), (1, PAD + LANES - STEPS)):
        for r in range(rows):
            side_out[k, pl.ds(r * STEPS, PAD), :] = near[
                pl.ds((r + STEPS) * PITCH + first, PAD), :
            ]
    guard(0, lambda: field_copy(2).start())
    guard(0, lambda: field_copy(3).start())
    for i in range(4, 8):
        dl, dn = WAYS[i]
        for d, at, count in spots:
            r = d - 1 if dl < 0 else rows - d
            first = PAD if dn < 0 else PAD + LANES - count
            corner_out[i - 4, pl.ds(at, PAD), :] = near[pl.ds((r + STEPS) * PITCH + first, PAD), :]
        guard(dl, lambda i=i: field_copy(i).start())

    for i, way in enumerate(WAYS):
        guard(-way[0], lambda i=i: coef_copy(i).wait_recv())
    weigh(rows, coefs, held)
    broaden(rows, held, 0, c0)
    broaden(rows, held, 1, k2)
    loads[4].wait()
    loads[5].wait()
    turn(off, weight, off_t, w_t)

    for i in (0, 1):
        guard(-WAYS[i][0], lambda i=i: field_copy(i).wait_recv())
        start = (STEPS + rows) if i == 0 else 0

        def far_row(r, carry, i=i, start=start):
            block = far_rows[i, aligned(r * layers, layers), :]
            near[aligned((r + start) * PITCH + PAD, LANES), :] = upright(block)
            return carry

        lax.fori_loop(0, STEPS, far_row, 0, unroll=2)
    for i in (2, 3):
        field_copy(i).wait_recv()
        for r in range(rows):
            base = (r + STEPS) * PITCH
            if i == 3:
                near[pl.ds(base, PAD), :] = side_in[1, pl.ds((r + 1) * STEPS, PAD), :]
            else:
                near[pl.ds(base + PAD + LANES, PAD), :] = side_in[0, pl.ds(PAD + r * STEPS, PAD), :]
    for i in range(4, 8):
        dl, dn = WAYS[i]
        guard(-dl, lambda i=i: field_copy(i).wait_recv())
        for d in range(1, STEPS + 1):
            at, count = spots[d - 1][1:] if d < STEPS else (0, 0)
            r = STEPS + rows + d - 1 if dl < 0 else STEPS - d
            if dn > 0:
                near[pl.ds(r * PITCH, PAD), :] = corner_in[i - 4, pl.ds(at + count, PAD), :]
            else:
                near[pl.ds(r * PITCH + PAD + LANES, PAD), :] = corner_in[i - 4, pl.ds(PAD + at, PAD), :]

    diffuse(rows, near, far, c0, k2)

    def back_row(r, carry):
        done[aligned(r * LANES, LANES), :] = near[aligned((r + STEPS) * PITCH + PAD, LANES), :].T
        return carry

    lax.fori_loop(0, rows, back_row, 0, unroll=2)
    loads[3].wait()
    solve_columns(rows, layers, done, control, coefs.at[1], vert, inc_ref)
    for i, way in enumerate(WAYS):
        guard(way[0], lambda i=i: coef_copy(i).wait_send())
        guard(way[0], lambda i=i: field_copy(i).wait_send())


def pick(table, row, col):
    level = [jnp.take_along_axis(t, col, axis=1) for t in table]
    bit = 1
    while len(level) > 1:
        odd = (row & bit) != 0
        level = [jnp.where(odd, level[i + 1], level[i]) for i in range(0, len(level), 2)]
        bit *= 2
    return level[0]


def lookup_kernel(rows, layers, owners, inc_ref, off_t, w_t, out_ref, acc):
    blocks = out_ref.shape[0] // owners
    cap = blocks * LANES
    groups = off_t.shape[0]
    turns = -(-cap // layers)

    def one_group(lg, carry):
        base = pl.multiple_of(lg * SUB, SUB)
        table = [inc_ref[pl.ds(base * rows + r, SUB, stride=rows), :] for r in range(rows)]
        for m in range(turns):
            at = pl.ds(m * layers + base, SUB)
            total = None
            for g in range(groups):
                idx = off_t[g, at, :]
                term = pick(table, idx >> 7, idx & (LANES - 1)) * w_t[g, at, :]
                total = term if total is None else total + term
            acc[at, :] = total
        return carry

    lax.fori_loop(0, layers // SUB, one_group, 0, unroll=2)
    for c in range(cap // LANES):
        here = pl.ds(c * LANES, LANES)
        block = acc[here, :].T
        total = block[:owners]
        for k in range(1, LANES // owners):
            total = total + block[k * owners : (k + 1) * owners]
        out_ref[pl.ds(c, owners, stride=blocks), :] = total


def local_call(kernel, shapes, count, scratch=(), name=None):
    return pl.pallas_call(
        kernel,
        out_shape=shapes,
        in_specs=[pl.BlockSpec(memory_space=pltpu.VMEM)] * count,
        out_specs=jax.tree.map(lambda _: pl.BlockSpec(memory_space=pltpu.VMEM), shapes),
        scratch_shapes=list(scratch),
        compiler_params=pltpu.CompilerParams(vmem_limit_bytes=40 * 1024 * 1024),
        name=name,
    )


def floats(*shape):
    return jax.ShapeDtypeStruct(shape, jnp.float32)


def columns_and_partials(control, kappa, sea_mask, vert_coef, offsets, weights):
    levels, fields, rows, cols = control.shape
    layers = levels * fields
    tall = rows + 2 * STEPS
    sten, owners, cap = offsets.shape
    bundles = sten * owners // LANES
    padded = -(-cap // layers) * layers
    corner = corner_spots()[1] + 2 * PAD
    vmem = pltpu.VMEM
    wide = (tall * PITCH, LANES)
    shapes = (
        floats(layers * rows, LANES),
        jax.ShapeDtypeStruct((bundles, padded, LANES), jnp.int32),
        floats(bundles, padded, LANES),
    )
    increment, off_t, w_t = pl.pallas_call(
        functools.partial(field_kernel, lax.axis_size("lat"), lax.axis_size("lon"), rows, layers),
        out_shape=shapes,
        in_specs=[pl.BlockSpec(memory_space=pl.ANY)] * 6,
        out_specs=tuple(pl.BlockSpec(memory_space=pltpu.VMEM) for _ in shapes),
        scratch_shapes=[
            vmem((layers * rows, LANES), jnp.float32),
            vmem((rows, LANES), jnp.float32),
            vmem((rows, LANES), jnp.int32),
            vmem((levels * rows, LANES), jnp.float32),
            vmem((sten * owners, cap), jnp.int32),
            vmem((sten * owners, cap), jnp.float32),
            vmem((3, 3 * rows, LANES), jnp.float32),
            vmem((2, 3, 40, LANES), jnp.float32),
            vmem((rows * layers, LANES), jnp.float32),
            vmem((2, STEPS * layers, LANES), jnp.float32),
            vmem((2, rows * STEPS + 2 * PAD, LANES), jnp.float32),
            vmem((2, rows * STEPS + 2 * PAD, LANES), jnp.float32),
            vmem((4, corner, LANES), jnp.float32),
            vmem((4, corner, LANES), jnp.float32),
            vmem(wide, jnp.float32),
            vmem(wide, jnp.float32),
            vmem(wide, jnp.float32),
            vmem(wide, jnp.float32),
            vmem((rows * LANES, LANES), jnp.float32),
            pltpu.SemaphoreType.DMA((6,)),
            pltpu.SemaphoreType.DMA((len(WAYS),)),
            pltpu.SemaphoreType.DMA((len(WAYS),)),
            pltpu.SemaphoreType.DMA((len(WAYS),)),
            pltpu.SemaphoreType.DMA((len(WAYS),)),
        ],
        compiler_params=pltpu.CompilerParams(
            vmem_limit_bytes=48 * 1024 * 1024, collective_id=2, has_side_effects=True
        ),
        name="field",
    )(
        control.reshape(layers * rows, cols),
        kappa,
        sea_mask,
        vert_coef.reshape(levels * rows, cols),
        offsets.reshape(sten * owners, cap),
        weights.reshape(sten * owners, cap),
    )
    partial_value = local_call(
        functools.partial(lookup_kernel, rows, layers, owners),
        floats(owners * cap // LANES, LANES),
        3,
        [vmem((padded, LANES), jnp.float32)],
        name="lookup",
    )(increment, off_t, w_t)
    return increment.reshape(control.shape), partial_value.reshape(owners, cap // LANES, LANES)


def spread(v, t, high):
    cap = v.shape[1]
    hit = lax.broadcasted_iota(jnp.int32, (high, cap), 0) == (t >> 7)
    ones = lax.broadcasted_iota(jnp.int32, (LANES, cap), 0) == (t & (LANES - 1))
    first = v.astype(jnp.bfloat16).astype(jnp.float32)
    left = jnp.concatenate(
        [jnp.where(hit, part, 0.0).astype(jnp.bfloat16) for part in (first, v - first)], axis=0
    )
    right = jnp.where(ones, 1.0, 0.0).astype(jnp.bfloat16)
    return lax.dot_general(
        left, right, (((1,), (1,)), ((), ())), preferred_element_type=jnp.float32
    )


def owner_kernel(n_lon, devices, part_ref, tgt_ref, obs_ref, err_ref, out_ref, recv, acc, send_sem, recv_sem):
    high = obs_ref.shape[0]
    blocks = part_ref.shape[1]
    me = lax.axis_index("lat") * n_lon + lax.axis_index("lon")

    def place(q):
        return (q // n_lon, q % n_lon)

    def copy(k):
        q = lax.rem(me + k, devices)
        return pltpu.make_async_remote_copy(
            src_ref=part_ref.at[q],
            dst_ref=recv.at[k],
            send_sem=send_sem.at[k],
            recv_sem=recv_sem.at[k],
            device_id=place(q),
            device_id_type=pl.DeviceIdType.MESH,
        )

    barrier = pltpu.get_barrier_semaphore()

    def greet(k, carry):
        q = lax.rem(me + k, devices)
        pl.semaphore_signal(
            barrier, inc=1, device_id=place(q), device_id_type=pl.DeviceIdType.MESH
        )
        return carry

    lax.fori_loop(1, devices, greet, 0)
    recv[0] = part_ref[me]
    acc[...] = jnp.zeros_like(acc)
    pl.semaphore_wait(barrier, devices - 1)

    def send(k, carry):
        copy(k).start()
        return carry

    lax.fori_loop(1, devices, send, 0)

    def add(k):
        p = lax.rem(me - k + devices, devices)
        cells = recv[k]
        v = jnp.concatenate([cells[c : c + 1, :] for c in range(blocks)], axis=1)
        acc[...] += spread(v, tgt_ref[pl.ds(p, 1), :], high)

    add(0)

    def one_source(k, carry):
        copy(k).wait_recv()
        add(k)
        return carry

    lax.fori_loop(1, devices, one_source, 0)

    def drain(k, carry):
        copy(k).wait_send()
        return carry

    lax.fori_loop(1, devices, drain, 0)
    out_ref[...] = (acc[:high] + acc[high:] - obs_ref[...]) * err_ref[...]


def owner_misfit(partial_value, target, observed, inv_error):
    high = observed.shape[0] // LANES
    devices, blocks, _ = partial_value.shape
    out = pl.pallas_call(
        functools.partial(owner_kernel, lax.axis_size("lon"), devices),
        out_shape=jax.ShapeDtypeStruct((high, LANES), jnp.float32),
        in_specs=[pl.BlockSpec(memory_space=pltpu.VMEM)] * 4,
        out_specs=pl.BlockSpec(memory_space=pltpu.VMEM),
        scratch_shapes=[
            pltpu.VMEM(partial_value.shape, jnp.float32),
            pltpu.VMEM((2 * high, LANES), jnp.float32),
            pltpu.SemaphoreType.DMA((devices,)),
            pltpu.SemaphoreType.DMA((devices,)),
        ],
        compiler_params=pltpu.CompilerParams(
            vmem_limit_bytes=32 * 1024 * 1024, collective_id=1, has_side_effects=True
        ),
        name="owner_misfit",
    )(partial_value, target, observed.reshape(high, LANES), inv_error.reshape(high, LANES))
    return out.reshape(-1)


def per_device(
    control,
    kappa,
    sea_mask,
    vert_coef,
    stencil_offsets,
    stencil_weights,
    slot_target,
    observed,
    inv_error,
):
    increment, partial_value = columns_and_partials(
        control, kappa, sea_mask, vert_coef, stencil_offsets, stencil_weights
    )
    misfit = owner_misfit(partial_value, slot_target, observed, inv_error)
    return (increment, misfit)


def solution(mesh):
    return jax.shard_map(
        per_device,
        mesh=mesh,
        in_specs=(
            P(None, None, "lat", "lon"),
            P("lat", "lon"),
            P("lat", "lon"),
            P(None, "lat", "lon"),
            P(None, ("lat", "lon"), None),
            P(None, ("lat", "lon"), None),
            P(("lat", "lon"), None),
            P(("lat", "lon")),
            P(("lat", "lon")),
        ),
        out_specs=(P(None, None, "lat", "lon"), P(("lat", "lon"))),
        check_vma=False,
    )
```

time: 74.1 us -> 52.8 us (0.71)
  starting transfers between devices: 10.6 us -> 0 us
  Pallas kernels: 54.8 us -> 44.5 us
  waiting for transfers between devices: 4.38 us -> 0 us
  local copies, waits for them, and re-layouts: 3.18 us -> 7.31 us
    ppermute x4 -> x0, starting transfers between devices: 10.6 us -> none  [shift(): return lax.ppermute(block, axis, pairs)]
    pallas_call x4 -> x2, Pallas kernels: 32.9 us -> 26.8 us  [the longest x1 21 us: columns_and_partials(): pl.pallas_call(functools.partial(field_kernel, lax.axis_size('lat'), lax....]
    ppermute x4 -> x0, waiting for transfers between devices: 4.38 us -> none  [shift(): return lax.ppermute(block, axis, pairs)]
    unnamed x19 -> x20, local copies, waits for them, and re-layouts: 3.12 us -> 7.31 us
    pallas_call x1, Pallas kernels: 21.8 us -> 17.7 us  [owner_misfit(): pl.pallas_call(functools.partial(owner_kernel, lax.axis_size('lon'), devi...]
  transfers between devices with their start and end apart: 4 -> 0, of which waited for: 3 -> 0; matrix products, arithmetic and copies ran while one was open for 0% -> 0% of each run, Pallas kernels for 1% -> 0%
where the time goes in v2:
time: 52.8 us; the launch traced here: 52.5 us
  Pallas kernels  44.5 us (84%)
  local copies, waits for them, and re-layouts  7.31 us (14%)
  between operations  0.72 us (1%)
    pallas_call x1, Pallas kernels, columns_and_partials(): pl.pallas_call(functools.partial(field_kernel, lax.axis_size('lat'), lax....  21 us
    pallas_call x1, Pallas kernels, owner_misfit(): pl.pallas_call(functools.partial(owner_kernel, lax.axis_size('lon'), devi...  17.7 us
    unnamed x20, local copies, waits for them, and re-layouts  7.31 us
    pallas_call x1, Pallas kernels, columns_and_partials(): local_call(functools.partial(lookup_kernel, rows, layers, owners), floats...  5.76 us

profile of v2, /device:TPU:0, one launch (start us, length us, event | category | flops | bytes accessed | tf_op | source)
XLA Modules:
  0.0 52.5 jit_solution(9284048841077197080)
XLA Ops:
  0.6 0.0 copy-start
  0.6 1.2 %copy-done = s32[8,32,1024]{2,1,0:T(8,128)S(1)} copy-done((s32[8,32,1024]{2,1,0:T(8,128)S(1)}, s32[8,32,1024]{2,1,0:T(8,128)}, u32[]{:S(2)}) %copy-start) | copy-done | bytes 1048600
  1.9 0.0 copy-start.1
  1.9 1.2 %copy-done.1 = f32[8,32,1024]{2,1,0:T(8,128)S(1)} copy-done((f32[8,32,1024]{2,1,0:T(8,128)S(1)}, f32[8,32,1024]{2,1,0:T(8,128)}, u32[]{:S(2)}) %copy-start.1) | copy-done | bytes 1048600
  3.1 0.0 copy-start.2
  3.1 1.1 %copy-done.2 = f32[20,4,16,128]{3,2,1,0:T(8,128)S(1)} copy-done((f32[20,4,16,128]{3,2,1,0:T(8,128)S(1)}, f32[20,4,16,128]{3,2,1,0:T(8,128)}, u32[]{:S(2)}) %copy-start.2) | copy-done | bytes 655384
  4.2 0.0 copy-start.3
  4.2 0.9 %copy-done.3 = f32[20,16,128]{2,1,0:T(8,128)S(1)} copy-done((f32[20,16,128]{2,1,0:T(8,128)S(1)}, f32[20,16,128]{2,1,0:T(8,128)}, u32[]{:S(2)}) %copy-start.3) | copy-done | bytes 163864
  5.1 0.0 copy-start.7
  5.1 0.7 %copy-done.7 = f32[16,128]{1,0:T(8,128)S(1)} copy-done((f32[16,128]{1,0:T(8,128)S(1)}, f32[16,128]{1,0:T(8,128)}, u32[]{:S(2)}) %copy-start.7) | copy-done | bytes 8216
  5.8 0.0 copy-start.8
  5.8 0.7 %copy-done.8 = s32[16,128]{1,0:T(8,128)S(1)} copy-done((s32[16,128]{1,0:T(8,128)S(1)}, s32[16,128]{1,0:T(8,128)}, u32[]{:S(2)}) %copy-start.8) | copy-done | bytes 8216
  6.5 21.0 %field.1 = (f32[1280,128]{1,0:T(8,128)S(1)}, s32[2,1040,128]{2,1,0:T(8,128)S(1)}, f32[2,1040,128]{2,1,0:T(8,128)S(1)}) custom-call(f32[1280,128]{1,0:T(8,128)S(1)} %bitcast.12, f32[16,128]{1,0:T(8,128)S(1)} %copy-done.7, s32[16,128]{1,0:T(8,128)S(1)} %copy-done.8, f32[320,128]{1,0:T(8,128)S(1)} %bitcast.14, s32[256,1024]{1,0:T(8,128)S(1)} %bitcast.10, ...), custom_call_target="tpu_custom_call" | custom-call | tf_op jit(solution)/shard_map/field/pallas_call | solution.py:417
  27.5 0.0 copy-start.4
  27.5 0.0 copy-start.5
  27.6 0.0 copy-start.6
  27.6 5.8 %lookup.1 = f32[256,128]{1,0:T(8,128)S(1)} custom-call(f32[1280,128]{1,0:T(8,128)S(1)} %get-tuple-element.5.inc_ref, s32[2,1040,128]{2,1,0:T(8,128)S(1)} %get-tuple-element.6.off_t, f32[2,1040,128]{2,1,0:T(8,128)S(1)} %get-tuple-element.7.w_t), custom_call_target="tpu_custom_call" | custom-call | tf_op jit(solution)/shard_map/lookup/pallas_call | solution.py:460
  33.3 0.0 copy-done.4
  33.3 0.0 copy-done.5
  33.4 0.0 copy-done.6
  33.4 17.7 %owner_misfit.1 = f32[64,128]{1,0:T(8,128)S(1)} custom-call(f32[32,8,128]{2,1,0:T(8,128)S(1)} %bitcast.13, s32[32,1024]{1,0:T(8,128)S(1)} %copy-done.4, f32[64,128]{1,0:T(8,128)S(1)} %bitcast.16, f32[64,128]{1,0:T(8,128)S(1)} %bitcast.17), custom_call_target="tpu_custom_call" | custom-call | tf_op jit(solution)/shard_map/owner_misfit/pallas_call | solution.py:549
  51.0 0.8 %copy.13 = f32[20,4,16,128]{3,2,1,0:T(8,128)} copy(f32[20,4,16,128]{3,2,1,0:T(8,128)S(1)} %bitcast.9) | data formatting | bytes 1310720
  51.9 0.6 %copy.14 = f32[8192]{0:T(1024)} copy(f32[8192]{0:T(1024)S(1)} %bitcast.15) | data formatting | bytes 65536
Async XLA Ops:
  0.6 1.2 %copy-start = (s32[8,32,1024]{2,1,0:T(8,128)S(1)}, s32[8,32,1024]{2,1,0:T(8,128)}, u32[]{:S(2)}) copy-start(s32[8,32,1024]{2,1,0:T(8,128)} %param.13) | copy-start | bytes 3145732
  1.9 1.2 %copy-start.1 = (f32[8,32,1024]{2,1,0:T(8,128)S(1)}, f32[8,32,1024]{2,1,0:T(8,128)}, u32[]{:S(2)}) copy-start(f32[8,32,1024]{2,1,0:T(8,128)} %param.14) | copy-start | bytes 3145732
  3.1 1.1 %copy-start.2 = (f32[20,4,16,128]{3,2,1,0:T(8,128)S(1)}, f32[20,4,16,128]{3,2,1,0:T(8,128)}, u32[]{:S(2)}) copy-start(f32[20,4,16,128]{3,2,1,0:T(8,128)} %param.9) | copy-start | bytes 1966084
  4.2 0.9 %copy-start.3 = (f32[20,16,128]{2,1,0:T(8,128)S(1)}, f32[20,16,128]{2,1,0:T(8,128)}, u32[]{:S(2)}) copy-start(f32[20,16,128]{2,1,0:T(8,128)} %param.12) | copy-start | bytes 491524
  5.1 0.7 %copy-start.7 = (f32[16,128]{1,0:T(8,128)S(1)}, f32[16,128]{1,0:T(8,128)}, u32[]{:S(2)}) copy-start(f32[16,128]{1,0:T(8,128)} %kappa_ref.1) | copy-start | bytes 24580
  5.8 0.7 %copy-start.8 = (s32[16,128]{1,0:T(8,128)S(1)}, s32[16,128]{1,0:T(8,128)}, u32[]{:S(2)}) copy-start(s32[16,128]{1,0:T(8,128)} %mask_ref.1) | copy-start | bytes 24580
  27.5 5.8 %copy-start.4 = (s32[32,1024]{1,0:T(8,128)S(1)}, s32[32,1024]{1,0:T(8,128)}, u32[]{:S(2)}) copy-start(s32[32,1024]{1,0:T(8,128)} %tgt_ref.1) | copy-start | bytes 393220
  27.5 5.8 %copy-start.5 = (f32[8192]{0:T(1024)S(1)}, f32[8192]{0:T(1024)}, u32[]{:S(2)}) copy-start(f32[8192]{0:T(1024)} %param.16) | copy-start | bytes 98308
  27.6 5.8 %copy-start.6 = (f32[8192]{0:T(1024)S(1)}, f32[8192]{0:T(1024)}, u32[]{:S(2)}) copy-start(f32[8192]{0:T(1024)} %param.17) | copy-start | bytes 98308

commit v3 on v2

--- a/solution.py
+++ b/solution.py
@@ -12,6 +12,8 @@
 SUB = 8
 
 
+CHUNKS = 2
+GROUP = 8
 WAYS = ((-1, 0), (1, 0), (0, -1), (0, 1), (-1, -1), (-1, 1), (1, -1), (1, 1))
 PAD = 16
 PITCH = LANES + 2 * PAD
@@ -140,7 +142,7 @@
             w_t[g, here, :] = w_ref[pl.ds(g * LANES, LANES), here].T
 
 
-def field_kernel(
+def step_kernel(
     n_lat,
     n_lon,
     rows,
@@ -151,15 +153,22 @@
     vert_ref,
     off_ref,
     w_ref,
+    target_ref,
     inc_ref,
-    off_t,
-    w_t,
+    value_ref,
     control,
     kappa,
     mask,
     vert,
     off,
     weight,
+    target,
+    off_t,
+    w_t,
+    acc,
+    parts,
+    received,
+    total,
     coefs,
     held,
     laid,
@@ -178,13 +187,16 @@
     coef_recv,
     send_sem,
     recv_sem,
+    part_send,
+    part_recv,
 ):
     lat, lon = lax.axis_index("lat"), lax.axis_index("lon")
+    me, devices = lat * n_lon + lon, n_lat * n_lon
     tall = rows + 2 * STEPS
     pairs = ((control_ref, control), (kappa_ref, kappa), (mask_ref, mask))
-    pairs += ((vert_ref, vert), (off_ref, off), (w_ref, weight))
+    pairs += ((vert_ref, vert), (off_ref, off), (w_ref, weight), (target_ref, target))
     loads = [pltpu.make_async_copy(a, b, load_sem.at[i]) for i, (a, b) in enumerate(pairs)]
-    for i in (1, 2, 0, 3, 4, 5):
+    for i in (1, 2, 0, 3, 4, 5, 6):
         loads[i].start()
 
     def place(i):
@@ -210,13 +222,17 @@
         far_rows[0] = jnp.zeros((STEPS * layers, LANES), jnp.float32)
 
     barrier = pltpu.get_barrier_semaphore()
-    for i, way in enumerate(WAYS):
-        guard(
-            way[0],
-            lambda i=i: pl.semaphore_signal(
-                barrier, inc=1, device_id=place(i), device_id_type=pl.DeviceIdType.MESH
-            ),
+    def owner(k):
+        q = lax.rem(me + k, devices)
+        return q, (q // n_lon, q % n_lon)
+
+    def greet(k, carry):
+        pl.semaphore_signal(
+            barrier, inc=1, device_id=owner(k)[1], device_id_type=pl.DeviceIdType.MESH
         )
+        return carry
+
+    lax.fori_loop(1, devices, greet, 0)
 
     def remote(i, src, dst, out_sem, in_sem):
         return pltpu.make_async_remote_copy(
@@ -253,8 +269,7 @@
     loads[1].wait()
     loads[2].wait()
     coefs[1, pl.ds(rows, rows), :] = kappa[...] * mask[...].astype(jnp.float32)
-    north, south = (lat > 0).astype(jnp.int32), (lat < n_lat - 1).astype(jnp.int32)
-    pl.semaphore_wait(barrier, 2 + 3 * (north + south))
+    pl.semaphore_wait(barrier, devices - 1)
     for i, way in enumerate(WAYS):
         guard(way[0], lambda i=i: coef_copy(i).start())
 
@@ -343,6 +358,67 @@
         guard(way[0], lambda i=i: coef_copy(i).wait_send())
         guard(way[0], lambda i=i: field_copy(i).wait_send())
 
+    def part_copy(c, k):
+        q, there = owner(k)
+        return pltpu.make_async_remote_copy(
+            src_ref=parts.at[c, q],
+            dst_ref=received.at[c, k],
+            send_sem=part_send.at[c, k],
+            recv_sem=part_recv.at[c, k],
+            device_id=there,
+            device_id_type=pl.DeviceIdType.MESH,
+        )
+
+    blocks, high = parts.shape[2], value_ref.shape[0]
+    size = blocks * LANES
+    turns = off_t.shape[1] // layers
+    done_turns = 0
+    total[...] = jnp.zeros_like(total)
+    for c in range(CHUNKS):
+        last = min(turns, -(-(c + 1) * size // layers))
+        lookup(rows, layers, range(done_turns, last), inc_ref, off_t, w_t, acc)
+        done_turns = last
+        for b in range(blocks):
+            block = acc[pl.ds(c * size + b * LANES, LANES), :].T
+            part = block[:devices]
+            for k in range(1, LANES // devices):
+                part = part + block[k * devices : (k + 1) * devices]
+            parts[c, :, b, :] = part
+        received[c, 0] = parts[c, me]
+
+        def send(k, carry, c=c):
+            part_copy(c, k).start()
+            return carry
+
+        lax.fori_loop(1, devices, send, 0)
+
+    loads[6].wait()
+    for c in range(CHUNKS):
+
+        def add_group(g, carry, c=c):
+            result = total[...]
+            for k in range(GROUP):
+                k = g * GROUP + k
+                pl.when(k > 0)(lambda k=k: part_copy(c, k).wait_recv())
+            for k in range(GROUP):
+                k = g * GROUP + k
+                p = lax.rem(me - k + devices, devices)
+                cells = received[c, k]
+                v = jnp.concatenate([cells[b : b + 1, :] for b in range(blocks)], axis=1)
+                result = result + spread(v, target[pl.ds(p, 1), c * size : (c + 1) * size], high)
+            total[...] = result
+            return carry
+
+        lax.fori_loop(0, devices // GROUP, add_group, 0)
+    value_ref[...] = total[:high] + total[high:]
+    for c in range(CHUNKS):
+
+        def drain(k, carry, c=c):
+            part_copy(c, k).wait_send()
+            return carry
+
+        lax.fori_loop(1, devices, drain, 0)
+
 
 def pick(table, row, col):
     level = [jnp.take_along_axis(t, col, axis=1) for t in table]
@@ -354,16 +430,13 @@
     return level[0]
 
 
-def lookup_kernel(rows, layers, owners, inc_ref, off_t, w_t, out_ref, acc):
-    blocks = out_ref.shape[0] // owners
-    cap = blocks * LANES
+def lookup(rows, layers, turns, inc_ref, off_t, w_t, acc):
     groups = off_t.shape[0]
-    turns = -(-cap // layers)
 
     def one_group(lg, carry):
         base = pl.multiple_of(lg * SUB, SUB)
         table = [inc_ref[pl.ds(base * rows + r, SUB, stride=rows), :] for r in range(rows)]
-        for m in range(turns):
+        for m in turns:
             at = pl.ds(m * layers + base, SUB)
             total = None
             for g in range(groups):
@@ -374,195 +447,31 @@
         return carry
 
     lax.fori_loop(0, layers // SUB, one_group, 0, unroll=2)
-    for c in range(cap // LANES):
-        here = pl.ds(c * LANES, LANES)
-        block = acc[here, :].T
-        total = block[:owners]
-        for k in range(1, LANES // owners):
-            total = total + block[k * owners : (k + 1) * owners]
-        out_ref[pl.ds(c, owners, stride=blocks), :] = total
-
-
-def local_call(kernel, shapes, count, scratch=(), name=None):
-    return pl.pallas_call(
-        kernel,
-        out_shape=shapes,
-        in_specs=[pl.BlockSpec(memory_space=pltpu.VMEM)] * count,
-        out_specs=jax.tree.map(lambda _: pl.BlockSpec(memory_space=pltpu.VMEM), shapes),
-        scratch_shapes=list(scratch),
-        compiler_params=pltpu.CompilerParams(vmem_limit_bytes=40 * 1024 * 1024),
-        name=name,
-    )
 
 
 def floats(*shape):
     return jax.ShapeDtypeStruct(shape, jnp.float32)
 
 
-def columns_and_partials(control, kappa, sea_mask, vert_coef, offsets, weights):
-    levels, fields, rows, cols = control.shape
-    layers = levels * fields
-    tall = rows + 2 * STEPS
-    sten, owners, cap = offsets.shape
-    bundles = sten * owners // LANES
-    padded = -(-cap // layers) * layers
-    corner = corner_spots()[1] + 2 * PAD
-    vmem = pltpu.VMEM
-    wide = (tall * PITCH, LANES)
-    shapes = (
-        floats(layers * rows, LANES),
-        jax.ShapeDtypeStruct((bundles, padded, LANES), jnp.int32),
-        floats(bundles, padded, LANES),
+def spread(v, t, high):
+    shape, bf = (high, v.shape[1]), jnp.bfloat16
+    flat = (LANES, v.shape[1])
+    upper = lax.broadcasted_iota(jnp.int32, shape, 0).astype(bf)
+    lower = lax.broadcasted_iota(jnp.int32, flat, 0).astype(bf)
+    hit = upper == jnp.broadcast_to((t >> 7).astype(jnp.float32), shape).astype(bf)
+    one = lower == jnp.broadcast_to((t & (LANES - 1)).astype(jnp.float32), flat).astype(bf)
+    first = v.astype(bf).astype(jnp.float32)
+    left = jnp.concatenate(
+        [
+            jnp.where(hit, jnp.broadcast_to(part, shape).astype(bf), jnp.zeros(shape, bf))
+            for part in (first, v - first)
+        ],
+        axis=0,
     )
-    increment, off_t, w_t = pl.pallas_call(
-        functools.partial(field_kernel, lax.axis_size("lat"), lax.axis_size("lon"), rows, layers),
-        out_shape=shapes,
-        in_specs=[pl.BlockSpec(memory_space=pl.ANY)] * 6,
-        out_specs=tuple(pl.BlockSpec(memory_space=pltpu.VMEM) for _ in shapes),
-        scratch_shapes=[
-            vmem((layers * rows, LANES), jnp.float32),
-            vmem((rows, LANES), jnp.float32),
-            vmem((rows, LANES), jnp.int32),
-            vmem((levels * rows, LANES), jnp.float32),
-            vmem((sten * owners, cap), jnp.int32),
-            vmem((sten * owners, cap), jnp.float32),
-            vmem((3, 3 * rows, LANES), jnp.float32),
-            vmem((2, 3, 40, LANES), jnp.float32),
-            vmem((rows * layers, LANES), jnp.float32),
-            vmem((2, STEPS * layers, LANES), jnp.float32),
-            vmem((2, rows * STEPS + 2 * PAD, LANES), jnp.float32),
-            vmem((2, rows * STEPS + 2 * PAD, LANES), jnp.float32),
-            vmem((4, corner, LANES), jnp.float32),
-            vmem((4, corner, LANES), jnp.float32),
-            vmem(wide, jnp.float32),
-            vmem(wide, jnp.float32),
-            vmem(wide, jnp.float32),
-            vmem(wide, jnp.float32),
-            vmem((rows * LANES, LANES), jnp.float32),
-            pltpu.SemaphoreType.DMA((6,)),
-            pltpu.SemaphoreType.DMA((len(WAYS),)),
-            pltpu.SemaphoreType.DMA((len(WAYS),)),
-            pltpu.SemaphoreType.DMA((len(WAYS),)),
-            pltpu.SemaphoreType.DMA((len(WAYS),)),
-        ],
-        compiler_params=pltpu.CompilerParams(
-            vmem_limit_bytes=48 * 1024 * 1024, collective_id=2, has_side_effects=True
-        ),
-        name="field",
-    )(
-        control.reshape(layers * rows, cols),
-        kappa,
-        sea_mask,
-        vert_coef.reshape(levels * rows, cols),
-        offsets.reshape(sten * owners, cap),
-        weights.reshape(sten * owners, cap),
-    )
-    partial_value = local_call(
-        functools.partial(lookup_kernel, rows, layers, owners),
-        floats(owners * cap // LANES, LANES),
-        3,
-        [vmem((padded, LANES), jnp.float32)],
-        name="lookup",
-    )(increment, off_t, w_t)
-    return increment.reshape(control.shape), partial_value.reshape(owners, cap // LANES, LANES)
-
-
-def spread(v, t, high):
-    cap = v.shape[1]
-    hit = lax.broadcasted_iota(jnp.int32, (high, cap), 0) == (t >> 7)
-    ones = lax.broadcasted_iota(jnp.int32, (LANES, cap), 0) == (t & (LANES - 1))
-    first = v.astype(jnp.bfloat16).astype(jnp.float32)
-    left = jnp.concatenate(
-        [jnp.where(hit, part, 0.0).astype(jnp.bfloat16) for part in (first, v - first)], axis=0
-    )
-    right = jnp.where(ones, 1.0, 0.0).astype(jnp.bfloat16)
+    right = jnp.where(one, jnp.ones(flat, bf), jnp.zeros(flat, bf))
     return lax.dot_general(
         left, right, (((1,), (1,)), ((), ())), preferred_element_type=jnp.float32
     )
-
-
-def owner_kernel(n_lon, devices, part_ref, tgt_ref, obs_ref, err_ref, out_ref, recv, acc, send_sem, recv_sem):
-    high = obs_ref.shape[0]
-    blocks = part_ref.shape[1]
-    me = lax.axis_index("lat") * n_lon + lax.axis_index("lon")
-
-    def place(q):
-        return (q // n_lon, q % n_lon)
-
-    def copy(k):
-        q = lax.rem(me + k, devices)
-        return pltpu.make_async_remote_copy(
-            src_ref=part_ref.at[q],
-            dst_ref=recv.at[k],
-            send_sem=send_sem.at[k],
-            recv_sem=recv_sem.at[k],
-            device_id=place(q),
-            device_id_type=pl.DeviceIdType.MESH,
-        )
-
-    barrier = pltpu.get_barrier_semaphore()
-
-    def greet(k, carry):
-        q = lax.rem(me + k, devices)
-        pl.semaphore_signal(
-            barrier, inc=1, device_id=place(q), device_id_type=pl.DeviceIdType.MESH
-        )
-        return carry
-
-    lax.fori_loop(1, devices, greet, 0)
-    recv[0] = part_ref[me]
-    acc[...] = jnp.zeros_like(acc)
-    pl.semaphore_wait(barrier, devices - 1)
-
-    def send(k, carry):
-        copy(k).start()
-        return carry
-
-    lax.fori_loop(1, devices, send, 0)
-
-    def add(k):
-        p = lax.rem(me - k + devices, devices)
-        cells = recv[k]
-        v = jnp.concatenate([cells[c : c + 1, :] for c in range(blocks)], axis=1)
-        acc[...] += spread(v, tgt_ref[pl.ds(p, 1), :], high)
-
-    add(0)
-
-    def one_source(k, carry):
-        copy(k).wait_recv()
-        add(k)
-        return carry
-
-    lax.fori_loop(1, devices, one_source, 0)
-
-    def drain(k, carry):
-        copy(k).wait_send()
-        return carry
-
-    lax.fori_loop(1, devices, drain, 0)
-    out_ref[...] = (acc[:high] + acc[high:] - obs_ref[...]) * err_ref[...]
-
-
-def owner_misfit(partial_value, target, observed, inv_error):
-    high = observed.shape[0] // LANES
-    devices, blocks, _ = partial_value.shape
-    out = pl.pallas_call(
-        functools.partial(owner_kernel, lax.axis_size("lon"), devices),
-        out_shape=jax.ShapeDtypeStruct((high, LANES), jnp.float32),
-        in_specs=[pl.BlockSpec(memory_space=pltpu.VMEM)] * 4,
-        out_specs=pl.BlockSpec(memory_space=pltpu.VMEM),
-        scratch_shapes=[
-            pltpu.VMEM(partial_value.shape, jnp.float32),
-            pltpu.VMEM((2 * high, LANES), jnp.float32),
-            pltpu.SemaphoreType.DMA((devices,)),
-            pltpu.SemaphoreType.DMA((devices,)),
-        ],
-        compiler_params=pltpu.CompilerParams(
-            vmem_limit_bytes=32 * 1024 * 1024, collective_id=1, has_side_effects=True
-        ),
-        name="owner_misfit",
-    )(partial_value, target, observed.reshape(high, LANES), inv_error.reshape(high, LANES))
-    return out.reshape(-1)
 
 
 def per_device(
@@ -576,11 +485,75 @@
     observed,
     inv_error,
 ):
-    increment, partial_value = columns_and_partials(
-        control, kappa, sea_mask, vert_coef, stencil_offsets, stencil_weights
+    levels, fields, rows, cols = control.shape
+    layers = levels * fields
+    tall = rows + 2 * STEPS
+    sten, owners, cap = stencil_offsets.shape
+    bundles = sten * owners // LANES
+    padded = -(-cap // layers) * layers
+    corner = corner_spots()[1] + 2 * PAD
+    high = observed.shape[0] // LANES
+    blocks = cap // LANES // CHUNKS
+
+    def vmem(*shape, dtype=jnp.float32):
+        return pltpu.VMEM(shape, dtype)
+
+    wide = (tall * PITCH, LANES)
+    dma = pltpu.SemaphoreType.DMA
+    increment, value = pl.pallas_call(
+        functools.partial(step_kernel, lax.axis_size("lat"), lax.axis_size("lon"), rows, layers),
+        out_shape=(floats(layers * rows, LANES), floats(high, LANES)),
+        in_specs=[pl.BlockSpec(memory_space=pltpu.HBM)] * 7,
+        out_specs=(pl.BlockSpec(memory_space=pltpu.VMEM), pl.BlockSpec(memory_space=pltpu.VMEM)),
+        scratch_shapes=[
+            vmem(layers * rows, LANES),
+            vmem(rows, LANES),
+            vmem(rows, LANES, dtype=jnp.int32),
+            vmem(levels * rows, LANES),
+            vmem(sten * owners, cap, dtype=jnp.int32),
+            vmem(sten * owners, cap),
+            vmem(owners, cap, dtype=jnp.int32),
+            vmem(bundles, padded, LANES, dtype=jnp.int32),
+            vmem(bundles, padded, LANES),
+            vmem(padded, LANES),
+            vmem(CHUNKS, owners, blocks, LANES),
+            vmem(CHUNKS, owners, blocks, LANES),
+            vmem(2 * high, LANES),
+            vmem(3, 3 * rows, LANES),
+            vmem(2, 3, 40, LANES),
+            vmem(rows * layers, LANES),
+            vmem(2, STEPS * layers, LANES),
+            vmem(2, rows * STEPS + 2 * PAD, LANES),
+            vmem(2, rows * STEPS + 2 * PAD, LANES),
+            vmem(4, corner, LANES),
+            vmem(4, corner, LANES),
+            vmem(*wide),
+            vmem(*wide),
+            vmem(*wide),
+            vmem(*wide),
+            vmem(rows * LANES, LANES),
+            dma((7,)),
+            dma((len(WAYS),)),
+            dma((len(WAYS),)),
+            dma((len(WAYS),)),
+            dma((len(WAYS),)),
+            dma((CHUNKS, owners)),
+            dma((CHUNKS, owners)),
+        ],
+        compiler_params=pltpu.CompilerParams(
+            vmem_limit_bytes=52 * 1024 * 1024, collective_id=2, has_side_effects=True
+        ),
+        name="assimilate",
+    )(
+        control.reshape(layers * rows, cols),
+        kappa,
+        sea_mask,
+        vert_coef.reshape(levels * rows, cols),
+        stencil_offsets.reshape(sten * owners, cap),
+        stencil_weights.reshape(sten * owners, cap),
+        slot_target,
     )
-    misfit = owner_misfit(partial_value, slot_target, observed, inv_error)
-    return (increment, misfit)
+    return increment.reshape(control.shape), (value.reshape(-1) - observed) * inv_error
 
 
 def solution(mesh):

time: 52.8 us -> 44.5 us (0.84)
  Pallas kernels: 44.5 us -> 37.8 us
  local copies, waits for them, and re-layouts: 7.31 us -> 5.14 us
  other arithmetic: 0 us -> 0.62 us
    pallas_call x3 -> x1, Pallas kernels: 44.5 us -> 37.8 us  [per_device(): pl.pallas_call(functools.partial(step_kernel, lax.axis_size('lat'), lax.a...]
    unnamed x20 -> x15, local copies, waits for them, and re-layouts: 7.31 us -> 5.14 us
    mul x0 -> x1, other arithmetic: none -> 0.62 us  [per_device(): (value.reshape(-1) - observed) * inv_error]
where the time goes in v3:
time: 44.5 us; the launch traced here: 44.2 us
  Pallas kernels  37.8 us (85%)
  local copies, waits for them, and re-layouts  5.14 us (12%)
  between operations  0.67 us (2%)
  other arithmetic  0.62 us (1%)
    pallas_call x1, Pallas kernels, per_device(): pl.pallas_call(functools.partial(step_kernel, lax.axis_size('lat'), lax.a...  37.8 us
    unnamed x15, local copies, waits for them, and re-layouts  5.14 us

profile of v3, /device:TPU:0, one launch (start us, length us, event | category | flops | bytes accessed | tf_op | source)
XLA Modules:
  0.0 44.2 jit_solution(2079785399291163070)
XLA Ops:
  0.6 0.0 copy-start
  0.6 1.1 %copy-done = f32[20,4,16,128]{3,2,1,0:T(8,128)S(1)} copy-done((f32[20,4,16,128]{3,2,1,0:T(8,128)S(1)}, f32[20,4,16,128]{3,2,1,0:T(8,128)}, u32[]{:S(2)}) %copy-start) | copy-done | bytes 655384
  1.7 0.0 copy-start.1
  1.7 0.9 %copy-done.1 = f32[20,16,128]{2,1,0:T(8,128)S(1)} copy-done((f32[20,16,128]{2,1,0:T(8,128)S(1)}, f32[20,16,128]{2,1,0:T(8,128)}, u32[]{:S(2)}) %copy-start.1) | copy-done | bytes 163864
  2.6 0.0 copy-start.2
  2.6 0.9 %copy-done.2 = s32[32,1024]{1,0:T(8,128)S(1)} copy-done((s32[32,1024]{1,0:T(8,128)S(1)}, s32[32,1024]{1,0:T(8,128)}, u32[]{:S(2)}) %copy-start.2) | copy-done | bytes 131096
  3.5 0.0 copy-start.3
  3.5 0.7 %copy-done.3 = f32[16,128]{1,0:T(8,128)S(1)} copy-done((f32[16,128]{1,0:T(8,128)S(1)}, f32[16,128]{1,0:T(8,128)}, u32[]{:S(2)}) %copy-start.3) | copy-done | bytes 8216
  4.2 0.0 copy-start.4
  4.2 0.7 %copy-done.4 = s32[16,128]{1,0:T(8,128)S(1)} copy-done((s32[16,128]{1,0:T(8,128)S(1)}, s32[16,128]{1,0:T(8,128)}, u32[]{:S(2)}) %copy-start.4) | copy-done | bytes 8216
  4.9 0.0 copy-start.5
  4.9 0.0 copy-start.6
  4.9 37.8 %assimilate.1 = (f32[1280,128]{1,0:T(8,128)S(1)}, f32[64,128]{1,0:T(8,128)S(1)}) custom-call(f32[1280,128]{1,0:T(8,128)S(1)} %bitcast.10, f32[16,128]{1,0:T(8,128)S(1)} %copy-done.3, s32[16,128]{1,0:T(8,128)S(1)} %copy-done.4, f32[320,128]{1,0:T(8,128)S(1)} %bitcast.11, s32[256,1024]{1,0:T(8,128)} %bitcast.12, f32[256,1024]{1,0:T(8,128)} %bitcast.13, ...), custom_call_target="tpu_custom_call" | custom-call | tf_op jit(solution)/shard_map/assimilate/pallas_call | solution.py:503
  42.8 0.0 copy-done.5
  42.8 0.0 copy-done.6
  42.8 0.6 %fusion = f32[8192]{0:T(1024)} fusion(f32[8192]{0:T(1024)S(1)} %copy-done.5, f32[8192]{0:T(1024)S(1)} %copy-done.6, f32[64,128]{1,0:T(8,128)S(1)} %get-tuple-element.5), kind=kLoop, calls=%fused_computation.1 | loop fusion | flops 16384 | bytes 131072 | tf_op jit(solution)/shard_map/mul | solution.py:556
  43.4 0.8 %copy.12 = f32[20,4,16,128]{3,2,1,0:T(8,128)} copy(f32[20,4,16,128]{3,2,1,0:T(8,128)S(1)} %bitcast.9) | data formatting | bytes 1310720
Async XLA Ops:
  0.6 1.1 %copy-start = (f32[20,4,16,128]{3,2,1,0:T(8,128)S(1)}, f32[20,4,16,128]{3,2,1,0:T(8,128)}, u32[]{:S(2)}) copy-start(f32[20,4,16,128]{3,2,1,0:T(8,128)} %param.9) | copy-start | bytes 1966084
  1.7 0.9 %copy-start.1 = (f32[20,16,128]{2,1,0:T(8,128)S(1)}, f32[20,16,128]{2,1,0:T(8,128)}, u32[]{:S(2)}) copy-start(f32[20,16,128]{2,1,0:T(8,128)} %param.12) | copy-start | bytes 491524
  2.6 0.9 %copy-start.2 = (s32[32,1024]{1,0:T(8,128)S(1)}, s32[32,1024]{1,0:T(8,128)}, u32[]{:S(2)}) copy-start(s32[32,1024]{1,0:T(8,128)} %target_ref.1) | copy-start | bytes 393220
  3.5 0.7 %copy-start.3 = (f32[16,128]{1,0:T(8,128)S(1)}, f32[16,128]{1,0:T(8,128)}, u32[]{:S(2)}) copy-start(f32[16,128]{1,0:T(8,128)} %kappa_ref.1) | copy-start | bytes 24580
  4.2 0.7 %copy-start.4 = (s32[16,128]{1,0:T(8,128)S(1)}, s32[16,128]{1,0:T(8,128)}, u32[]{:S(2)}) copy-start(s32[16,128]{1,0:T(8,128)} %mask_ref.1) | copy-start | bytes 24580
  4.9 37.8 %copy-start.5 = (f32[8192]{0:T(1024)S(1)}, f32[8192]{0:T(1024)}, u32[]{:S(2)}) copy-start(f32[8192]{0:T(1024)} %param.17) | copy-start | bytes 98308
  4.9 37.8 %copy-start.6 = (f32[8192]{0:T(1024)S(1)}, f32[8192]{0:T(1024)}, u32[]{:S(2)}) copy-start(f32[8192]{0:T(1024)} %param.16) | copy-start | bytes 98308

commit v4 on v3

--- a/solution.py
+++ b/solution.py
@@ -12,7 +12,6 @@
 SUB = 8
 
 
-CHUNKS = 2
 GROUP = 8
 WAYS = ((-1, 0), (1, 0), (0, -1), (0, 1), (-1, -1), (-1, 1), (1, -1), (1, 1))
 PAD = 16
@@ -31,32 +30,48 @@
     return spots, -(-at // SUB) * SUB
 
 
-def update(old, new, c0, k2, count, first, low, high):
-    def two_rows(turn, carry):
-        base = (first + 2 * turn) * PITCH
+def corner_split():
+    count = STEPS * (STEPS - 1) // 2
+    return count - count // 3, count // 3
+
+
+def side_split(rows):
+    return (rows - rows // 3) * STEPS, rows // 3 * STEPS
+
+
+def message(kept, few):
+    return max(-(-kept // SUB), -(-few // SUB) + -(-few // SUB)) * SUB
+
+
+def update(old, new, c0, k2, count, first, low, high, per):
+    def some_rows(turn, carry):
+        base = (first + per * turn) * PITCH
         for v in range(low, high):
-            spot = [aligned(base + d * PITCH + v * SUB, SUB) for d in range(-1, 3)]
+            spot = [aligned(base + d * PITCH + v * SUB, SUB) for d in range(-1, per + 1)]
             cells = [old[s, :] for s in spot]
-            for d in range(2):
+            for d in range(per):
                 at = base + d * PITCH + v * SUB
                 side = old[pl.ds(at - 1, SUB), :] + old[pl.ds(at + 1, SUB), :]
                 around = (cells[d] + cells[d + 2]) + side
                 new[spot[d + 1], :] = c0[spot[d + 1], :] * cells[d + 1] + k2[spot[d + 1], :] * around
         return carry
 
-    lax.fori_loop(0, count, two_rows, 0)
+    lax.fori_loop(0, count, some_rows, 0)
 
 
 def diffuse(rows, old, new, c0, k2):
     tall = rows + 2 * STEPS
     width = PITCH // SUB
-    update(old, new, c0, k2, (tall - 2) // 2, 1, 0, width)
-    update(new, old, c0, k2, (tall - 4) // 2, 2, 1, width - 1)
+    fours = (tall - 2) // 4
+    update(old, new, c0, k2, fours, 1, 0, width, 4)
+    if (tall - 2) % 4:
+        update(old, new, c0, k2, 1, 1 + 4 * fours, 0, width, 2)
+    update(new, old, c0, k2, -(-(tall - 4) // 4), 2, 1, width - 1, 4)
 
     def two_steps(s, carry):
         first = 2 * s + 1
-        update(old, new, c0, k2, (tall - 2 * first) // 2, first, 1, width - 1)
-        update(new, old, c0, k2, (tall - 2 * first - 2) // 2, first + 1, 1, width - 1)
+        update(old, new, c0, k2, (tall - 2 * first + 2) // 4, first, 1, width - 1, 4)
+        update(new, old, c0, k2, (tall - 2 * first) // 4, first + 1, 1, width - 1, 4)
         return carry
 
     lax.fori_loop(1, STEPS // 2, two_steps, 0)
@@ -127,19 +142,43 @@
         out[pl.ds(base + PAD + LANES, PAD), :] = jnp.broadcast_to(column[:PAD], (PAD, LANES))
 
 
-def turn(off_ref, w_ref, off_t, w_t):
+def turn(owners, off_ref, w_ref, off_t, w_t):
     cap = off_ref.shape[1]
-    groups = off_ref.shape[0] // LANES
+    sten = off_ref.shape[0] // owners
+    members = LANES // sten
     padded = off_t.shape[1]
-    if padded > cap:
-        for g in range(groups):
+    for g in range(owners // members):
+        if padded > cap:
             off_t[g, cap:padded, :] = jnp.zeros((padded - cap, LANES), jnp.int32)
             w_t[g, cap:padded, :] = jnp.zeros((padded - cap, LANES), jnp.float32)
-    for g in range(groups):
         for c in range(cap // LANES):
             here = pl.ds(c * LANES, LANES)
-            off_t[g, here, :] = off_ref[pl.ds(g * LANES, LANES), here].T
-            w_t[g, here, :] = w_ref[pl.ds(g * LANES, LANES), here].T
+            for src, dst in ((off_ref, off_t), (w_ref, w_t)):
+                dst[g, here, :] = jnp.concatenate(
+                    [src[pl.ds(j * owners + g * members, members), here] for j in range(sten)], axis=0
+                ).T
+
+
+def squeeze(layers, kept, few, src, dst):
+    spare = LANES - layers
+    size = -(-few // SUB) * SUB
+    whole = dst.shape[0]
+    lane = lax.broadcasted_iota(jnp.int32, (size, LANES), 1)
+    dst[...] = src[pl.ds(0, whole), :]
+    rest = src[pl.ds(kept, size), :]
+    dst[pl.ds(0, size), :] = jnp.where(lane < layers, src[pl.ds(0, size), :], rest)
+    moved = pltpu.roll(rest, layers - spare, 1)
+    dst[pl.ds(few, size), :] = jnp.where(lane < layers, src[pl.ds(few, size), :], moved)
+
+
+def unsqueeze(layers, kept, few, src, dst):
+    spare = LANES - layers
+    size = -(-few // SUB) * SUB
+    lane = lax.broadcasted_iota(jnp.int32, (size, LANES), 1)
+    dst[pl.ds(PAD, src.shape[0]), :] = src[...]
+    first = pltpu.roll(src[pl.ds(0, size), :], spare, 1)
+    second = pltpu.roll(src[pl.ds(few, size), :], LANES - layers + spare, 1)
+    dst[pl.ds(PAD + kept, size), :] = jnp.where(lane < spare, first, second)
 
 
 def step_kernel(
@@ -177,6 +216,10 @@
     side_in,
     corner_out,
     corner_in,
+    side_sent,
+    side_got,
+    corner_sent,
+    corner_got,
     near,
     far,
     c0,
@@ -208,6 +251,20 @@
         else:
             pl.when(lat > 0 if step < 0 else lat < n_lat - 1)(body)
 
+    corner_got[...] = jnp.zeros_like(corner_got)
+    barrier = pltpu.get_barrier_semaphore()
+    def owner(k):
+        q = lax.rem(me + k, devices)
+        return q, (q // n_lon, q % n_lon)
+
+    def greet(k, carry):
+        pl.semaphore_signal(
+            barrier, inc=1, device_id=owner(k)[1], device_id_type=pl.DeviceIdType.MESH
+        )
+        return carry
+
+    lax.fori_loop(1, devices, greet, 0)
+
     side_in[...] = jnp.zeros_like(side_in)
     corner_in[...] = jnp.zeros_like(corner_in)
 
@@ -220,19 +277,6 @@
     def _():
         coefs[:, 2 * rows :, :] = jnp.zeros((3, rows, LANES), jnp.float32)
         far_rows[0] = jnp.zeros((STEPS * layers, LANES), jnp.float32)
-
-    barrier = pltpu.get_barrier_semaphore()
-    def owner(k):
-        q = lax.rem(me + k, devices)
-        return q, (q // n_lon, q % n_lon)
-
-    def greet(k, carry):
-        pl.semaphore_signal(
-            barrier, inc=1, device_id=owner(k)[1], device_id_type=pl.DeviceIdType.MESH
-        )
-        return carry
-
-    lax.fori_loop(1, devices, greet, 0)
 
     def remote(i, src, dst, out_sem, in_sem):
         return pltpu.make_async_remote_copy(
@@ -250,7 +294,7 @@
             i, coefs.at[1, pl.ds(rows, rows)], coefs.at[1 - dn, pl.ds((1 - dl) * rows, rows)], coef_send, coef_recv
         )
 
-    spots, corner_size = corner_spots()
+    spots = corner_spots()[0]
 
     def field_copy(i):
         dl, dn = WAYS[i]
@@ -259,20 +303,14 @@
             src = laid.at[pl.ds(start, STEPS * layers)]
             dst = far_rows.at[i]
         elif dl == 0:
-            src = side_out.at[i - 2, pl.ds(0, rows * STEPS)]
-            dst = side_in.at[i - 2, pl.ds(PAD, rows * STEPS)]
+            src, dst = side_sent.at[i - 2], side_got.at[i - 2]
         else:
-            src = corner_out.at[i - 4, pl.ds(0, corner_size)]
-            dst = corner_in.at[i - 4, pl.ds(PAD, corner_size)]
+            src, dst = corner_sent.at[i - 4], corner_got.at[i - 4]
         return remote(i, src, dst, send_sem, recv_sem)
 
     loads[1].wait()
     loads[2].wait()
     coefs[1, pl.ds(rows, rows), :] = kappa[...] * mask[...].astype(jnp.float32)
-    pl.semaphore_wait(barrier, devices - 1)
-    for i, way in enumerate(WAYS):
-        guard(way[0], lambda i=i: coef_copy(i).start())
-
     loads[0].wait()
     for r in range(rows):
         here = coefs[1, pl.ds(rows + r, 1), :]
@@ -280,9 +318,6 @@
             laid[pl.ds(r * layers + g * SUB, SUB), :] = (
                 control[pl.ds(g * SUB * rows + r, SUB, stride=rows), :] * here
             )
-    guard(-1, lambda: field_copy(0).start())
-    guard(1, lambda: field_copy(1).start())
-
     def upright(block):
         return jnp.concatenate([block, block[: LANES - layers]], axis=0).T
 
@@ -297,15 +332,19 @@
             side_out[k, pl.ds(r * STEPS, PAD), :] = near[
                 pl.ds((r + STEPS) * PITCH + first, PAD), :
             ]
-    guard(0, lambda: field_copy(2).start())
-    guard(0, lambda: field_copy(3).start())
+        squeeze(layers, *side_split(rows), side_out.at[k], side_sent.at[k])
     for i in range(4, 8):
         dl, dn = WAYS[i]
         for d, at, count in spots:
             r = d - 1 if dl < 0 else rows - d
             first = PAD if dn < 0 else PAD + LANES - count
             corner_out[i - 4, pl.ds(at, PAD), :] = near[pl.ds((r + STEPS) * PITCH + first, PAD), :]
-        guard(dl, lambda i=i: field_copy(i).start())
+        squeeze(layers, *corner_split(), corner_out.at[i - 4], corner_sent.at[i - 4])
+    pl.semaphore_wait(barrier, devices - 1)
+    for i, way in enumerate(WAYS):
+        guard(way[0], lambda i=i: coef_copy(i).start())
+    for i in (2, 3, 0, 1, 4, 5, 6, 7):
+        guard(WAYS[i][0], lambda i=i: field_copy(i).start())
 
     for i, way in enumerate(WAYS):
         guard(-way[0], lambda i=i: coef_copy(i).wait_recv())
@@ -314,7 +353,7 @@
     broaden(rows, held, 1, k2)
     loads[4].wait()
     loads[5].wait()
-    turn(off, weight, off_t, w_t)
+    turn(devices, off, weight, off_t, w_t)
 
     for i in (0, 1):
         guard(-WAYS[i][0], lambda i=i: field_copy(i).wait_recv())
@@ -328,6 +367,7 @@
         lax.fori_loop(0, STEPS, far_row, 0, unroll=2)
     for i in (2, 3):
         field_copy(i).wait_recv()
+        unsqueeze(layers, *side_split(rows), side_got.at[i - 2], side_in.at[i - 2])
         for r in range(rows):
             base = (r + STEPS) * PITCH
             if i == 3:
@@ -337,6 +377,7 @@
     for i in range(4, 8):
         dl, dn = WAYS[i]
         guard(-dl, lambda i=i: field_copy(i).wait_recv())
+        unsqueeze(layers, *corner_split(), corner_got.at[i - 4], corner_in.at[i - 4])
         for d in range(1, STEPS + 1):
             at, count = spots[d - 1][1:] if d < STEPS else (0, 0)
             r = STEPS + rows + d - 1 if dl < 0 else STEPS - d
@@ -358,66 +399,75 @@
         guard(way[0], lambda i=i: coef_copy(i).wait_send())
         guard(way[0], lambda i=i: field_copy(i).wait_send())
 
-    def part_copy(c, k):
-        q, there = owner(k)
+    passes, padded = off_t.shape[0], off_t.shape[1]
+    members = devices // passes
+    mine, local = me // members, me % members
+    blocks, high = parts.shape[2], value_ref.shape[0]
+
+    def toward(t):
+        return lax.rem(mine + t + 1, passes)
+
+    def part_copy(t, i):
+        there = lax.rem(local + i, members)
+        q = toward(t) * members + there
         return pltpu.make_async_remote_copy(
-            src_ref=parts.at[c, q],
-            dst_ref=received.at[c, k],
-            send_sem=part_send.at[c, k],
-            recv_sem=part_recv.at[c, k],
-            device_id=there,
+            src_ref=parts.at[t, there],
+            dst_ref=received.at[t, i],
+            send_sem=part_send.at[t, i],
+            recv_sem=part_recv.at[t, i],
+            device_id=(q // n_lon, q % n_lon),
             device_id_type=pl.DeviceIdType.MESH,
         )
 
-    blocks, high = parts.shape[2], value_ref.shape[0]
-    size = blocks * LANES
-    turns = off_t.shape[1] // layers
-    done_turns = 0
+    def apart(t, i):
+        return jnp.logical_or(t < passes - 1, i > 0)
+
+    def look_up(t, carry):
+        lookup(rows, layers, padded // layers, inc_ref, off_t.at[toward(t)], w_t.at[toward(t)], acc)
+        for b in range(blocks):
+            block = acc[pl.ds(b * LANES, LANES), :].T
+            part = block[:members]
+            for k in range(1, LANES // members):
+                part = part + block[k * members : (k + 1) * members]
+            parts[t, :, b, :] = part
+
+        def send(i, carry):
+            pl.when(apart(t, i))(lambda: part_copy(t, i).start())
+            return carry
+
+        lax.fori_loop(0, members, send, 0)
+        return carry
+
     total[...] = jnp.zeros_like(total)
-    for c in range(CHUNKS):
-        last = min(turns, -(-(c + 1) * size // layers))
-        lookup(rows, layers, range(done_turns, last), inc_ref, off_t, w_t, acc)
-        done_turns = last
-        for b in range(blocks):
-            block = acc[pl.ds(c * size + b * LANES, LANES), :].T
-            part = block[:devices]
-            for k in range(1, LANES // devices):
-                part = part + block[k * devices : (k + 1) * devices]
-            parts[c, :, b, :] = part
-        received[c, 0] = parts[c, me]
-
-        def send(k, carry, c=c):
-            part_copy(c, k).start()
-            return carry
-
-        lax.fori_loop(1, devices, send, 0)
-
+    lax.fori_loop(0, passes, look_up, 0)
+    received[passes - 1, 0] = parts[passes - 1, local]
     loads[6].wait()
-    for c in range(CHUNKS):
-
-        def add_group(g, carry, c=c):
-            result = total[...]
-            for k in range(GROUP):
-                k = g * GROUP + k
-                pl.when(k > 0)(lambda k=k: part_copy(c, k).wait_recv())
-            for k in range(GROUP):
-                k = g * GROUP + k
-                p = lax.rem(me - k + devices, devices)
-                cells = received[c, k]
-                v = jnp.concatenate([cells[b : b + 1, :] for b in range(blocks)], axis=1)
-                result = result + spread(v, target[pl.ds(p, 1), c * size : (c + 1) * size], high)
-            total[...] = result
-            return carry
-
-        lax.fori_loop(0, devices // GROUP, add_group, 0)
+
+    def add_group(turn, carry):
+        t, g = turn // (members // GROUP), turn % (members // GROUP)
+        result = total[...]
+        source = lax.rem(mine + passes - t - 1, passes) * members
+        for k in range(GROUP):
+            i = g * GROUP + k
+            pl.when(apart(t, i))(lambda i=i: part_copy(t, i).wait_recv())
+        for k in range(GROUP):
+            i = g * GROUP + k
+            p = source + lax.rem(local - i + members, members)
+            cells = received[t, i]
+            v = jnp.concatenate([cells[b : b + 1, :] for b in range(blocks)], axis=1)
+            result = result + spread(v, target[pl.ds(p, 1), :], high)
+        total[...] = result
+        return carry
+
+    lax.fori_loop(0, devices // GROUP, add_group, 0)
     value_ref[...] = total[:high] + total[high:]
-    for c in range(CHUNKS):
-
-        def drain(k, carry, c=c):
-            part_copy(c, k).wait_send()
-            return carry
-
-        lax.fori_loop(1, devices, drain, 0)
+
+    def drain(turn, carry):
+        t, i = turn // members, turn % members
+        pl.when(apart(t, i))(lambda: part_copy(t, i).wait_send())
+        return carry
+
+    lax.fori_loop(0, devices, drain, 0)
 
 
 def pick(table, row, col):
@@ -431,19 +481,13 @@
 
 
 def lookup(rows, layers, turns, inc_ref, off_t, w_t, acc):
-    groups = off_t.shape[0]
-
     def one_group(lg, carry):
         base = pl.multiple_of(lg * SUB, SUB)
         table = [inc_ref[pl.ds(base * rows + r, SUB, stride=rows), :] for r in range(rows)]
-        for m in turns:
+        for m in range(turns):
             at = pl.ds(m * layers + base, SUB)
-            total = None
-            for g in range(groups):
-                idx = off_t[g, at, :]
-                term = pick(table, idx >> 7, idx & (LANES - 1)) * w_t[g, at, :]
-                total = term if total is None else total + term
-            acc[at, :] = total
+            idx = off_t[at, :]
+            acc[at, :] = pick(table, idx >> 7, idx & (LANES - 1)) * w_t[at, :]
         return carry
 
     lax.fori_loop(0, layers // SUB, one_group, 0, unroll=2)
@@ -493,7 +537,8 @@
     padded = -(-cap // layers) * layers
     corner = corner_spots()[1] + 2 * PAD
     high = observed.shape[0] // LANES
-    blocks = cap // LANES // CHUNKS
+    blocks = cap // LANES
+    members = owners // bundles
 
     def vmem(*shape, dtype=jnp.float32):
         return pltpu.VMEM(shape, dtype)
@@ -516,8 +561,8 @@
             vmem(bundles, padded, LANES, dtype=jnp.int32),
             vmem(bundles, padded, LANES),
             vmem(padded, LANES),
-            vmem(CHUNKS, owners, blocks, LANES),
-            vmem(CHUNKS, owners, blocks, LANES),
+            vmem(bundles, members, blocks, LANES),
+            vmem(bundles, members, blocks, LANES),
             vmem(2 * high, LANES),
             vmem(3, 3 * rows, LANES),
             vmem(2, 3, 40, LANES),
@@ -527,6 +572,10 @@
             vmem(2, rows * STEPS + 2 * PAD, LANES),
             vmem(4, corner, LANES),
             vmem(4, corner, LANES),
+            vmem(2, message(*side_split(rows)), LANES),
+            vmem(2, message(*side_split(rows)), LANES),
+            vmem(4, message(*corner_split()), LANES),
+            vmem(4, message(*corner_split()), LANES),
             vmem(*wide),
             vmem(*wide),
             vmem(*wide),
@@ -537,21 +586,26 @@
             dma((len(WAYS),)),
             dma((len(WAYS),)),
             dma((len(WAYS),)),
-            dma((CHUNKS, owners)),
-            dma((CHUNKS, owners)),
+            dma((bundles, members)),
+            dma((bundles, members)),
         ],
         compiler_params=pltpu.CompilerParams(
             vmem_limit_bytes=52 * 1024 * 1024, collective_id=2, has_side_effects=True
         ),
         name="assimilate",
     )(
-        control.reshape(layers * rows, cols),
-        kappa,
-        sea_mask,
-        vert_coef.reshape(levels * rows, cols),
-        stencil_offsets.reshape(sten * owners, cap),
-        stencil_weights.reshape(sten * owners, cap),
-        slot_target,
+        *[
+            pltpu.with_memory_space_constraint(a, pltpu.HBM)
+            for a in (
+                control.reshape(layers * rows, cols),
+                kappa,
+                sea_mask,
+                vert_coef.reshape(levels * rows, cols),
+                stencil_offsets.reshape(sten * owners, cap),
+                stencil_weights.reshape(sten * owners, cap),
+                slot_target,
+            )
+        ]
     )
     return increment.reshape(control.shape), (value.reshape(-1) - observed) * inv_error
 

time: 44.5 us -> 37.7 us (0.85)
  local copies, waits for them, and re-layouts: 5.14 us -> 0.84 us
  Pallas kernels: 37.8 us -> 35.4 us
    unnamed x15 -> x5, local copies, waits for them, and re-layouts: 5.14 us -> 0.84 us
    pallas_call x1, Pallas kernels: 37.8 us -> 35.4 us  [per_device(): pl.pallas_call(functools.partial(step_kernel, lax.axis_size('lat'), lax.a...]
where the time goes in v4:
time: 37.7 us; the launch traced here: 37.5 us
  Pallas kernels  35.4 us (94%)
  local copies, waits for them, and re-layouts  0.84 us (2%)
  between operations  0.67 us (2%)
  other arithmetic  0.62 us (2%)
    pallas_call x1, Pallas kernels, per_device(): pl.pallas_call(functools.partial(step_kernel, lax.axis_size('lat'), lax.a...  35.4 us
    unnamed x5, local copies, waits for them, and re-layouts  0.84 us

profile of v4, /device:TPU:0, one launch (start us, length us, event | category | flops | bytes accessed | tf_op | source)
XLA Modules:
  0.0 37.5 jit_solution(3304154487026962969)
XLA Ops:
  0.6 0.0 copy-start
  0.6 0.0 copy-start.1
  0.7 35.4 %assimilate.1 = (f32[1280,128]{1,0:T(8,128)S(1)}, f32[64,128]{1,0:T(8,128)S(1)}) custom-call(f32[1280,128]{1,0:T(8,128)} %bitcast.12, f32[16,128]{1,0:T(8,128)} %kappa_ref.1, s32[16,128]{1,0:T(8,128)} %mask_ref.1, f32[320,128]{1,0:T(8,128)} %bitcast.13, s32[256,1024]{1,0:T(8,128)} %bitcast.10, f32[256,1024]{1,0:T(8,128)} %bitcast.11, s32[32,1024]{1,0:T(8,128)} %target_ref.1), custom_call_target="tpu_custom_call" | custom-call | tf_op jit(solution)/shard_map/assimilate/pallas_call | solution.py:548
  36.0 0.0 copy-done
  36.1 0.0 copy-done.1
  36.1 0.6 %fusion = f32[8192]{0:T(1024)} fusion(f32[8192]{0:T(1024)S(1)} %copy-done, f32[8192]{0:T(1024)S(1)} %copy-done.1, f32[64,128]{1,0:T(8,128)S(1)} %get-tuple-element.5), kind=kLoop, calls=%fused_computation.1 | loop fusion | flops 16384 | bytes 131072 | tf_op jit(solution)/shard_map/mul | solution.py:610
  36.7 0.8 %copy.12 = f32[20,4,16,128]{3,2,1,0:T(8,128)} copy(f32[20,4,16,128]{3,2,1,0:T(8,128)S(1)} %bitcast.9) | data formatting | bytes 1310720
Async XLA Ops:
  0.6 35.4 %copy-start = (f32[8192]{0:T(1024)S(1)}, f32[8192]{0:T(1024)}, u32[]{:S(2)}) copy-start(f32[8192]{0:T(1024)} %param.17) | copy-start | bytes 98308
  0.6 35.4 %copy-start.1 = (f32[8192]{0:T(1024)S(1)}, f32[8192]{0:T(1024)}, u32[]{:S(2)}) copy-start(f32[8192]{0:T(1024)} %param.16) | copy-start | bytes 98308

commit v5 on v4

--- a/solution.py
+++ b/solution.py
@@ -59,14 +59,26 @@
     lax.fori_loop(0, count, some_rows, 0)
 
 
-def diffuse(rows, old, new, c0, k2):
+def span(old, new, c0, k2, first, count, low, high):
+    per = 5 if count % 5 == 0 else 4
+    update(old, new, c0, k2, count // per, first, low, high, per)
+    if count % per:
+        update(old, new, c0, k2, 1, first + count // per * per, low, high, count % per)
+
+
+def diffuse_inner(rows, old, new, c0, k2):
+    width = PITCH // SUB
+    span(old, new, c0, k2, STEPS + 1, rows - 2, 0, width)
+    span(new, old, c0, k2, STEPS + 2, rows - 4, 1, width - 1)
+
+
+def diffuse_rest(rows, old, new, c0, k2):
     tall = rows + 2 * STEPS
     width = PITCH // SUB
-    fours = (tall - 2) // 4
-    update(old, new, c0, k2, fours, 1, 0, width, 4)
-    if (tall - 2) % 4:
-        update(old, new, c0, k2, 1, 1 + 4 * fours, 0, width, 2)
-    update(new, old, c0, k2, -(-(tall - 4) // 4), 2, 1, width - 1, 4)
+    for first in (1, STEPS + rows - 1):
+        span(old, new, c0, k2, first, STEPS, 0, width)
+    for first in (2, STEPS + rows - 2):
+        span(new, old, c0, k2, first, STEPS, 1, width - 1)
 
     def two_steps(s, carry):
         first = 2 * s + 1
@@ -77,25 +89,33 @@
     lax.fori_loop(1, STEPS // 2, two_steps, 0)
 
 
-def solve_columns(rows, layers, done, control, coef, vert_ref, inc_ref):
-    levels = vert_ref.shape[0] // rows
+def factor(rows, vert, inverse, ratio):
+    levels = vert.shape[0] // rows
+    above = vert[pl.ds(0, rows), :]
+    cprev = jnp.zeros((rows, LANES), jnp.float32)
+    for k in range(levels):
+        if k + 1 < levels:
+            below = vert[pl.ds((k + 1) * rows, rows), :]
+        else:
+            below = jnp.zeros((rows, LANES), jnp.float32)
+        inv = 1.0 / (((1.0 + above) + below) + above * cprev)
+        cprev = -below * inv
+        inverse[pl.ds(k * rows, rows), :] = inv
+        ratio[pl.ds(k * rows, rows), :] = cprev
+        above = below
+
+
+def solve_columns(rows, layers, done, control, coef, vert, inverse, ratio, inc_ref):
+    levels = vert.shape[0] // rows
     fields = layers // levels
     for h in range(rows // SUB):
         here = coef[pl.ds(rows + h * SUB, SUB), :]
         sea = here != 0.0
         back = 1.0 / jnp.where(sea, here, 1.0)
-        ratio = []
-        above = vert_ref[pl.ds(h * SUB, SUB), :]
-        cprev = jnp.zeros((SUB, LANES), jnp.float32)
-        prev = [cprev] * fields
+        prev = [jnp.zeros((SUB, LANES), jnp.float32)] * fields
         for k in range(levels):
-            if k + 1 < levels:
-                below = vert_ref[pl.ds((k + 1) * rows + h * SUB, SUB), :]
-            else:
-                below = jnp.zeros((SUB, LANES), jnp.float32)
-            inv = 1.0 / (((1.0 + above) + below) + above * cprev)
-            cprev = -below * inv
-            ratio.append(cprev)
+            level = pl.ds(k * rows + h * SUB, SUB)
+            above, inv = vert[level, :], inverse[level, :]
             for f in range(fields):
                 layer = k * fields + f
                 at = pl.ds(layer * rows + h * SUB, SUB)
@@ -103,11 +123,11 @@
                 right = jnp.where(sea, right, control[at, :])
                 prev[f] = (right + above * prev[f]) * inv
                 inc_ref[at, :] = prev[f]
-            above = below
         for k in range(levels - 2, -1, -1):
+            fall = ratio[pl.ds(k * rows + h * SUB, SUB), :]
             for f in range(fields):
                 at = pl.ds((k * fields + f) * rows + h * SUB, SUB)
-                prev[f] = inc_ref[at, :] - ratio[k] * prev[f]
+                prev[f] = inc_ref[at, :] - fall * prev[f]
                 inc_ref[at, :] = prev[f]
 
 
@@ -142,21 +162,30 @@
         out[pl.ds(base + PAD + LANES, PAD), :] = jnp.broadcast_to(column[:PAD], (PAD, LANES))
 
 
-def turn(owners, off_ref, w_ref, off_t, w_t):
-    cap = off_ref.shape[1]
-    sten = off_ref.shape[0] // owners
-    members = LANES // sten
-    padded = off_t.shape[1]
-    for g in range(owners // members):
+def turn(n_lat, n_lon, off, weight, off_t, w_t):
+    blocks, height, _ = off.shape
+    cap, padded = blocks * LANES, off_t.shape[1]
+    width = n_lon // off_t.shape[0]
+    ways = SUB // width
+    row = lax.broadcasted_iota(jnp.int32, (SUB, LANES), 0) // width
+
+    def gather(src, c, g):
+        tiles = []
+        for start in range(0, height, n_lon * ways):
+            tile = src[c, pl.ds(start + g * width, SUB), :]
+            for k in range(1, ways):
+                piece = src[c, pl.ds(start + k * n_lon + g * width - k * width, SUB), :]
+                tile = jnp.where(row == k, piece, tile)
+            tiles.append(tile)
+        return jnp.concatenate(tiles, axis=0).T
+
+    for g in range(off_t.shape[0]):
         if padded > cap:
             off_t[g, cap:padded, :] = jnp.zeros((padded - cap, LANES), jnp.int32)
             w_t[g, cap:padded, :] = jnp.zeros((padded - cap, LANES), jnp.float32)
-        for c in range(cap // LANES):
-            here = pl.ds(c * LANES, LANES)
-            for src, dst in ((off_ref, off_t), (w_ref, w_t)):
-                dst[g, here, :] = jnp.concatenate(
-                    [src[pl.ds(j * owners + g * members, members), here] for j in range(sten)], axis=0
-                ).T
+        for c in range(blocks):
+            off_t[g, pl.ds(c * LANES, LANES), :] = gather(off, c, g)
+            w_t[g, pl.ds(c * LANES, LANES), :] = gather(weight, c, g)
 
 
 def squeeze(layers, kept, few, src, dst):
@@ -181,7 +210,7 @@
     dst[pl.ds(PAD + kept, size), :] = jnp.where(lane < spare, first, second)
 
 
-def step_kernel(
+def field_kernel(
     n_lat,
     n_lon,
     rows,
@@ -192,22 +221,17 @@
     vert_ref,
     off_ref,
     w_ref,
-    target_ref,
     inc_ref,
-    value_ref,
+    off_t,
+    w_t,
     control,
     kappa,
     mask,
     vert,
     off,
     weight,
-    target,
-    off_t,
-    w_t,
-    acc,
-    parts,
-    received,
-    total,
+    inverse,
+    ratio,
     coefs,
     held,
     laid,
@@ -230,16 +254,16 @@
     coef_recv,
     send_sem,
     recv_sem,
-    part_send,
-    part_recv,
 ):
     lat, lon = lax.axis_index("lat"), lax.axis_index("lon")
-    me, devices = lat * n_lon + lon, n_lat * n_lon
     tall = rows + 2 * STEPS
     pairs = ((control_ref, control), (kappa_ref, kappa), (mask_ref, mask))
-    pairs += ((vert_ref, vert), (off_ref, off), (w_ref, weight), (target_ref, target))
+    pairs += ((vert_ref, vert),)
+    for c in range(off.shape[0]):
+        here = pl.ds(c * LANES, LANES)
+        pairs += ((off_ref.at[:, here], off.at[c]), (w_ref.at[:, here], weight.at[c]))
     loads = [pltpu.make_async_copy(a, b, load_sem.at[i]) for i, (a, b) in enumerate(pairs)]
-    for i in (1, 2, 0, 3, 4, 5, 6):
+    for i in (1, 2, 0, *range(3, len(loads))):
         loads[i].start()
 
     def place(i):
@@ -253,17 +277,13 @@
 
     corner_got[...] = jnp.zeros_like(corner_got)
     barrier = pltpu.get_barrier_semaphore()
-    def owner(k):
-        q = lax.rem(me + k, devices)
-        return q, (q // n_lon, q % n_lon)
-
-    def greet(k, carry):
-        pl.semaphore_signal(
-            barrier, inc=1, device_id=owner(k)[1], device_id_type=pl.DeviceIdType.MESH
+    for i, way in enumerate(WAYS):
+        guard(
+            way[0],
+            lambda i=i: pl.semaphore_signal(
+                barrier, inc=1, device_id=place(i), device_id_type=pl.DeviceIdType.MESH
+            ),
         )
-        return carry
-
-    lax.fori_loop(1, devices, greet, 0)
 
     side_in[...] = jnp.zeros_like(side_in)
     corner_in[...] = jnp.zeros_like(corner_in)
@@ -340,7 +360,8 @@
             first = PAD if dn < 0 else PAD + LANES - count
             corner_out[i - 4, pl.ds(at, PAD), :] = near[pl.ds((r + STEPS) * PITCH + first, PAD), :]
         squeeze(layers, *corner_split(), corner_out.at[i - 4], corner_sent.at[i - 4])
-    pl.semaphore_wait(barrier, devices - 1)
+    beside = (lat > 0).astype(jnp.int32) + (lat < n_lat - 1).astype(jnp.int32)
+    pl.semaphore_wait(barrier, 2 + 3 * beside)
     for i, way in enumerate(WAYS):
         guard(way[0], lambda i=i: coef_copy(i).start())
     for i in (2, 3, 0, 1, 4, 5, 6, 7):
@@ -351,20 +372,11 @@
     weigh(rows, coefs, held)
     broaden(rows, held, 0, c0)
     broaden(rows, held, 1, k2)
-    loads[4].wait()
-    loads[5].wait()
-    turn(devices, off, weight, off_t, w_t)
-
-    for i in (0, 1):
-        guard(-WAYS[i][0], lambda i=i: field_copy(i).wait_recv())
-        start = (STEPS + rows) if i == 0 else 0
-
-        def far_row(r, carry, i=i, start=start):
-            block = far_rows[i, aligned(r * layers, layers), :]
-            near[aligned((r + start) * PITCH + PAD, LANES), :] = upright(block)
-            return carry
-
-        lax.fori_loop(0, STEPS, far_row, 0, unroll=2)
+    for i in range(3, len(loads)):
+        loads[i].wait()
+    turn(n_lat, n_lon, off, weight, off_t, w_t)
+    factor(rows, vert, inverse, ratio)
+
     for i in (2, 3):
         field_copy(i).wait_recv()
         unsqueeze(layers, *side_split(rows), side_got.at[i - 2], side_in.at[i - 2])
@@ -386,88 +398,28 @@
             else:
                 near[pl.ds(r * PITCH + PAD + LANES, PAD), :] = corner_in[i - 4, pl.ds(PAD + at, PAD), :]
 
-    diffuse(rows, near, far, c0, k2)
+    diffuse_inner(rows, near, far, c0, k2)
+    for i in (0, 1):
+        guard(-WAYS[i][0], lambda i=i: field_copy(i).wait_recv())
+        start = (STEPS + rows) if i == 0 else 0
+
+        def far_row(r, carry, i=i, start=start):
+            block = far_rows[i, aligned(r * layers, layers), :]
+            near[aligned((r + start) * PITCH + PAD, LANES), :] = upright(block)
+            return carry
+
+        lax.fori_loop(0, STEPS, far_row, 0, unroll=2)
+    diffuse_rest(rows, near, far, c0, k2)
 
     def back_row(r, carry):
         done[aligned(r * LANES, LANES), :] = near[aligned((r + STEPS) * PITCH + PAD, LANES), :].T
         return carry
 
     lax.fori_loop(0, rows, back_row, 0, unroll=2)
-    loads[3].wait()
-    solve_columns(rows, layers, done, control, coefs.at[1], vert, inc_ref)
+    solve_columns(rows, layers, done, control, coefs.at[1], vert, inverse, ratio, inc_ref)
     for i, way in enumerate(WAYS):
         guard(way[0], lambda i=i: coef_copy(i).wait_send())
         guard(way[0], lambda i=i: field_copy(i).wait_send())
-
-    passes, padded = off_t.shape[0], off_t.shape[1]
-    members = devices // passes
-    mine, local = me // members, me % members
-    blocks, high = parts.shape[2], value_ref.shape[0]
-
-    def toward(t):
-        return lax.rem(mine + t + 1, passes)
-
-    def part_copy(t, i):
-        there = lax.rem(local + i, members)
-        q = toward(t) * members + there
-        return pltpu.make_async_remote_copy(
-            src_ref=parts.at[t, there],
-            dst_ref=received.at[t, i],
-            send_sem=part_send.at[t, i],
-            recv_sem=part_recv.at[t, i],
-            device_id=(q // n_lon, q % n_lon),
-            device_id_type=pl.DeviceIdType.MESH,
-        )
-
-    def apart(t, i):
-        return jnp.logical_or(t < passes - 1, i > 0)
-
-    def look_up(t, carry):
-        lookup(rows, layers, padded // layers, inc_ref, off_t.at[toward(t)], w_t.at[toward(t)], acc)
-        for b in range(blocks):
-            block = acc[pl.ds(b * LANES, LANES), :].T
-            part = block[:members]
-            for k in range(1, LANES // members):
-                part = part + block[k * members : (k + 1) * members]
-            parts[t, :, b, :] = part
-
-        def send(i, carry):
-            pl.when(apart(t, i))(lambda: part_copy(t, i).start())
-            return carry
-
-        lax.fori_loop(0, members, send, 0)
-        return carry
-
-    total[...] = jnp.zeros_like(total)
-    lax.fori_loop(0, passes, look_up, 0)
-    received[passes - 1, 0] = parts[passes - 1, local]
-    loads[6].wait()
-
-    def add_group(turn, carry):
-        t, g = turn // (members // GROUP), turn % (members // GROUP)
-        result = total[...]
-        source = lax.rem(mine + passes - t - 1, passes) * members
-        for k in range(GROUP):
-            i = g * GROUP + k
-            pl.when(apart(t, i))(lambda i=i: part_copy(t, i).wait_recv())
-        for k in range(GROUP):
-            i = g * GROUP + k
-            p = source + lax.rem(local - i + members, members)
-            cells = received[t, i]
-            v = jnp.concatenate([cells[b : b + 1, :] for b in range(blocks)], axis=1)
-            result = result + spread(v, target[pl.ds(p, 1), :], high)
-        total[...] = result
-        return carry
-
-    lax.fori_loop(0, devices // GROUP, add_group, 0)
-    value_ref[...] = total[:high] + total[high:]
-
-    def drain(turn, carry):
-        t, i = turn // members, turn % members
-        pl.when(apart(t, i))(lambda: part_copy(t, i).wait_send())
-        return carry
-
-    lax.fori_loop(0, devices, drain, 0)
 
 
 def pick(table, row, col):
@@ -490,7 +442,119 @@
             acc[at, :] = pick(table, idx >> 7, idx & (LANES - 1)) * w_t[at, :]
         return carry
 
-    lax.fori_loop(0, layers // SUB, one_group, 0, unroll=2)
+    lax.fori_loop(0, layers // SUB, one_group, 0, unroll=5)
+
+
+def observe_kernel(
+    n_lat,
+    n_lon,
+    rows,
+    layers,
+    inc_ref,
+    off_t,
+    w_t,
+    target_ref,
+    value_ref,
+    target,
+    acc,
+    parts,
+    received,
+    total,
+    load_sem,
+    part_send,
+    part_recv,
+):
+    lat, lon = lax.axis_index("lat"), lax.axis_index("lon")
+    me, devices = lat * n_lon + lon, n_lat * n_lon
+    passes, padded = off_t.shape[0], off_t.shape[1]
+    members, width = devices // passes, n_lon // passes
+    mine, local = lon // width, lat * width + lon % width
+    blocks, high = parts.shape[1], value_ref.shape[0]
+    load = pltpu.make_async_copy(target_ref, target, load_sem.at[0])
+    load.start()
+    barrier = pltpu.get_barrier_semaphore()
+
+    def greet(k, carry):
+        q = lax.rem(me + k, devices)
+        pl.semaphore_signal(
+            barrier, inc=1, device_id=(q // n_lon, q % n_lon), device_id_type=pl.DeviceIdType.MESH
+        )
+        return carry
+
+    lax.fori_loop(1, devices, greet, 0)
+
+    def toward(t):
+        return lax.rem(mine + t + 1, passes)
+
+    def slots(t, i, count=1):
+        return pl.ds(t * members + i, count)
+
+    def copy(src, dst, in_sem, there):
+        return pltpu.make_async_remote_copy(
+            src_ref=src,
+            dst_ref=dst,
+            send_sem=part_send.at[0],
+            recv_sem=in_sem,
+            device_id=there,
+            device_id_type=pl.DeviceIdType.MESH,
+        )
+
+    def part_copy(t, i):
+        there = lax.rem(local + i, members)
+        place = (there // width, toward(t) * width + there % width)
+        src, dst = parts.at[slots(t, there)], received.at[slots(t, i)]
+        return copy(src, dst, part_recv.at[t, i // GROUP], place)
+
+    def wait_group(t, g, first, count):
+        here = slots(t, g * GROUP + first, count)
+        copy(parts.at[here], received.at[here], part_recv.at[t, g], (lat, lon)).wait_recv()
+
+    def look_up(t, carry):
+        lookup(rows, layers, padded // layers, inc_ref, off_t.at[toward(t)], w_t.at[toward(t)], acc)
+        for b in range(blocks):
+            block = acc[pl.ds(b * LANES, LANES), :].T
+            part = block[:members]
+            for k in range(1, LANES // members):
+                part = part + block[k * members : (k + 1) * members]
+            parts[slots(t, 0, members), b, :] = part
+
+        @pl.when(t == 0)
+        def _():
+            pl.semaphore_wait(barrier, devices - 1)
+
+        def send(i, carry):
+            part_copy(t, i).start()
+            return carry
+
+        lax.fori_loop((t == passes - 1).astype(jnp.int32), members, send, 0)
+        return carry
+
+    total[...] = jnp.zeros_like(total)
+    lax.fori_loop(0, passes, look_up, 0)
+    received[slots(passes - 1, 0)] = parts[slots(passes - 1, local)]
+    load.wait()
+
+    def add_group(turn, carry):
+        t, g = turn // (members // GROUP), turn % (members // GROUP)
+        result = total[...]
+        source = lax.rem(mine + passes - t - 1, passes) * width
+        own = jnp.logical_and(t == passes - 1, g == 0)
+        pl.when(own)(lambda: wait_group(t, g, 1, GROUP - 1))
+        pl.when(jnp.logical_not(own))(lambda: wait_group(t, g, 0, GROUP))
+        for k in range(GROUP):
+            i = g * GROUP + k
+            p = lax.rem(local - i + members, members)
+            p = p // width * n_lon + source + p % width
+            cells = received[t * members + i]
+            v = jnp.concatenate([cells[b : b + 1, :] for b in range(blocks)], axis=1)
+            result = result + spread(v, target[pl.ds(p, 1), :], high)
+        total[...] = result
+        return carry
+
+    lax.fori_loop(0, devices // GROUP, add_group, 0)
+    value_ref[...] = total[:high] + total[high:]
+    sent = pl.ds(0, devices - 1)
+    copy(parts.at[sent], received.at[sent], part_recv.at[0, 0], (lat, lon)).wait_send()
 
 
 def floats(*shape):
@@ -545,25 +609,34 @@
 
     wide = (tall * PITCH, LANES)
     dma = pltpu.SemaphoreType.DMA
-    increment, value = pl.pallas_call(
-        functools.partial(step_kernel, lax.axis_size("lat"), lax.axis_size("lon"), rows, layers),
-        out_shape=(floats(layers * rows, LANES), floats(high, LANES)),
-        in_specs=[pl.BlockSpec(memory_space=pltpu.HBM)] * 7,
-        out_specs=(pl.BlockSpec(memory_space=pltpu.VMEM), pl.BlockSpec(memory_space=pltpu.VMEM)),
+    place = (lax.axis_size("lat"), lax.axis_size("lon"))
+    shapes = (
+        floats(layers * rows, LANES),
+        jax.ShapeDtypeStruct((bundles, padded, LANES), jnp.int32),
+        floats(bundles, padded, LANES),
+    )
+    arrays = (
+        control.reshape(layers * rows, cols),
+        kappa,
+        sea_mask,
+        vert_coef.reshape(levels * rows, cols),
+        stencil_offsets.reshape(sten * owners, cap),
+        stencil_weights.reshape(sten * owners, cap),
+    )
+    increment, off_t, w_t = pl.pallas_call(
+        functools.partial(field_kernel, *place, rows, layers),
+        out_shape=shapes,
+        in_specs=[pl.BlockSpec(memory_space=pltpu.HBM)] * len(arrays),
+        out_specs=tuple(pl.BlockSpec(memory_space=pltpu.VMEM) for _ in shapes),
         scratch_shapes=[
             vmem(layers * rows, LANES),
             vmem(rows, LANES),
             vmem(rows, LANES, dtype=jnp.int32),
             vmem(levels * rows, LANES),
-            vmem(sten * owners, cap, dtype=jnp.int32),
-            vmem(sten * owners, cap),
-            vmem(owners, cap, dtype=jnp.int32),
-            vmem(bundles, padded, LANES, dtype=jnp.int32),
-            vmem(bundles, padded, LANES),
-            vmem(padded, LANES),
-            vmem(bundles, members, blocks, LANES),
-            vmem(bundles, members, blocks, LANES),
-            vmem(2 * high, LANES),
+            vmem(blocks, sten * owners, LANES, dtype=jnp.int32),
+            vmem(blocks, sten * owners, LANES),
+            vmem(levels * rows, LANES),
+            vmem(levels * rows, LANES),
             vmem(3, 3 * rows, LANES),
             vmem(2, 3, 40, LANES),
             vmem(rows * layers, LANES),
@@ -581,32 +654,38 @@
             vmem(*wide),
             vmem(*wide),
             vmem(rows * LANES, LANES),
-            dma((7,)),
+            dma((4 + 2 * blocks,)),
             dma((len(WAYS),)),
             dma((len(WAYS),)),
             dma((len(WAYS),)),
             dma((len(WAYS),)),
-            dma((bundles, members)),
-            dma((bundles, members)),
         ],
         compiler_params=pltpu.CompilerParams(
-            vmem_limit_bytes=52 * 1024 * 1024, collective_id=2, has_side_effects=True
+            vmem_limit_bytes=44 * 1024 * 1024, collective_id=2, has_side_effects=True
         ),
-        name="assimilate",
-    )(
-        *[
-            pltpu.with_memory_space_constraint(a, pltpu.HBM)
-            for a in (
-                control.reshape(layers * rows, cols),
-                kappa,
-                sea_mask,
-                vert_coef.reshape(levels * rows, cols),
-                stencil_offsets.reshape(sten * owners, cap),
-                stencil_weights.reshape(sten * owners, cap),
-                slot_target,
-            )
-        ]
-    )
+        name="field",
+    )(*[pltpu.with_memory_space_constraint(a, pltpu.HBM) for a in arrays])
+    vm = pl.BlockSpec(memory_space=pltpu.VMEM)
+    value = pl.pallas_call(
+        functools.partial(observe_kernel, *place, rows, layers),
+        out_shape=floats(high, LANES),
+        in_specs=[vm, vm, vm, pl.BlockSpec(memory_space=pltpu.HBM)],
+        out_specs=vm,
+        scratch_shapes=[
+            vmem(owners, cap, dtype=jnp.int32),
+            vmem(padded, LANES),
+            vmem(owners, blocks, LANES),
+            vmem(owners, blocks, LANES),
+            vmem(2 * high, LANES),
+            dma((1,)),
+            dma((1,)),
+            dma((bundles, members // GROUP)),
+        ],
+        compiler_params=pltpu.CompilerParams(
+            vmem_limit_bytes=24 * 1024 * 1024, collective_id=3, has_side_effects=True
+        ),
+        name="observe",
+    )(increment, off_t, w_t, pltpu.with_memory_space_constraint(slot_target, pltpu.HBM))
     return increment.reshape(control.shape), (value.reshape(-1) - observed) * inv_error
 
 

time: 37.7 us -> 36.9 us (0.979)
  Pallas kernels: 35.4 us -> 34.5 us
    pallas_call x1 -> x2, Pallas kernels: 35.4 us -> 34.5 us  [the longest x1 21.3 us: per_device(): pl.pallas_call(functools.partial(field_kernel, *place, rows, layers), out...]
where the time goes in v5:
time: 36.9 us; the launch traced here: 36.7 us
  Pallas kernels  34.5 us (93%)
  local copies, waits for them, and re-layouts  0.85 us (2%)
  between operations  0.68 us (2%)
  other arithmetic  0.62 us (2%)
    pallas_call x1, Pallas kernels, per_device(): pl.pallas_call(functools.partial(field_kernel, *place, rows, layers), out...  21.3 us
    pallas_call x1, Pallas kernels, per_device(): pl.pallas_call(functools.partial(observe_kernel, *place, rows, layers), o...  13.2 us
    unnamed x5, local copies, waits for them, and re-layouts  0.85 us

profile of v5, /device:TPU:0, one launch (start us, length us, event | category | flops | bytes accessed | tf_op | source)
XLA Modules:
  0.0 36.7 jit_solution(4855386284534426303)
XLA Ops:
  0.6 21.3 %field.1 = (f32[1280,128]{1,0:T(8,128)S(1)}, s32[2,1040,128]{2,1,0:T(8,128)S(1)}, f32[2,1040,128]{2,1,0:T(8,128)S(1)}) custom-call(f32[1280,128]{1,0:T(8,128)} %bitcast.12, f32[16,128]{1,0:T(8,128)} %kappa_ref.1, s32[16,128]{1,0:T(8,128)} %mask_ref.1, f32[320,128]{1,0:T(8,128)} %bitcast.13, s32[256,1024]{1,0:T(8,128)} %bitcast.10, f32[256,1024]{1,0:T(8,128)} %bitcast.11), custom_call_target="tpu_custom_call" | custom-call | tf_op jit(solution)/shard_map/field/pallas_call | solution.py:626
  22.0 0.0 copy-start
  22.0 0.0 copy-start.1
  22.0 13.2 %observe.1 = f32[64,128]{1,0:T(8,128)S(1)} custom-call(f32[1280,128]{1,0:T(8,128)S(1)} %get-tuple-element.5.inc_ref, s32[2,1040,128]{2,1,0:T(8,128)S(1)} %get-tuple-element.6.off_t, f32[2,1040,128]{2,1,0:T(8,128)S(1)} %get-tuple-element.7.w_t, s32[32,1024]{1,0:T(8,128)} %target_ref.1), custom_call_target="tpu_custom_call" | custom-call | tf_op jit(solution)/shard_map/observe/pallas_call | solution.py:669
  35.2 0.0 copy-done
  35.2 0.0 copy-done.1
  35.2 0.6 %fusion = f32[8192]{0:T(1024)} fusion(f32[8192]{0:T(1024)S(1)} %copy-done, f32[8192]{0:T(1024)S(1)} %copy-done.1, f32[64,128]{1,0:T(8,128)S(1)} %observe.1), kind=kLoop, calls=%fused_computation.1 | loop fusion | flops 16384 | bytes 131072 | tf_op jit(solution)/shard_map/mul | solution.py:689
  35.8 0.8 %copy.12 = f32[20,4,16,128]{3,2,1,0:T(8,128)} copy(f32[20,4,16,128]{3,2,1,0:T(8,128)S(1)} %bitcast.9) | data formatting | bytes 1310720
Async XLA Ops:
  22.0 13.2 %copy-start = (f32[8192]{0:T(1024)S(1)}, f32[8192]{0:T(1024)}, u32[]{:S(2)}) copy-start(f32[8192]{0:T(1024)} %param.17) | copy-start | bytes 98308
  22.0 13.2 %copy-start.1 = (f32[8192]{0:T(1024)S(1)}, f32[8192]{0:T(1024)}, u32[]{:S(2)}) copy-start(f32[8192]{0:T(1024)} %param.16) | copy-start | bytes 98308

commit v6 on v5

--- a/solution.py
+++ b/solution.py
@@ -298,12 +298,12 @@
         coefs[:, 2 * rows :, :] = jnp.zeros((3, rows, LANES), jnp.float32)
         far_rows[0] = jnp.zeros((STEPS * layers, LANES), jnp.float32)
 
-    def remote(i, src, dst, out_sem, in_sem):
+    def remote(i, src, dst, out_sem, in_sem, part=0):
         return pltpu.make_async_remote_copy(
             src_ref=src,
             dst_ref=dst,
-            send_sem=out_sem.at[i],
-            recv_sem=in_sem.at[i],
+            send_sem=out_sem.at[i + part * len(WAYS)],
+            recv_sem=in_sem.at[i + part * len(WAYS)],
             device_id=place(i),
             device_id_type=pl.DeviceIdType.MESH,
         )
@@ -316,17 +316,19 @@
 
     spots = corner_spots()[0]
 
-    def field_copy(i):
+    half = STEPS // 2 * layers
+
+    def field_copy(i, part=0):
         dl, dn = WAYS[i]
         if dn == 0:
             start = 0 if dl < 0 else (rows - STEPS) * layers
-            src = laid.at[pl.ds(start, STEPS * layers)]
-            dst = far_rows.at[i]
+            src = laid.at[pl.ds(start + part * half, half)]
+            dst = far_rows.at[i, pl.ds(part * half, half)]
         elif dl == 0:
             src, dst = side_sent.at[i - 2], side_got.at[i - 2]
         else:
             src, dst = corner_sent.at[i - 4], corner_got.at[i - 4]
-        return remote(i, src, dst, send_sem, recv_sem)
+        return remote(i, src, dst, send_sem, recv_sem, part)
 
     loads[1].wait()
     loads[2].wait()
@@ -366,16 +368,18 @@
         guard(way[0], lambda i=i: coef_copy(i).start())
     for i in (2, 3, 0, 1, 4, 5, 6, 7):
         guard(WAYS[i][0], lambda i=i: field_copy(i).start())
-
+    for i in (0, 1):
+        guard(WAYS[i][0], lambda i=i: field_copy(i, 1).start())
+
+    for i in range(3, len(loads)):
+        loads[i].wait()
+    turn(n_lat, n_lon, off, weight, off_t, w_t)
+    factor(rows, vert, inverse, ratio)
     for i, way in enumerate(WAYS):
         guard(-way[0], lambda i=i: coef_copy(i).wait_recv())
     weigh(rows, coefs, held)
     broaden(rows, held, 0, c0)
     broaden(rows, held, 1, k2)
-    for i in range(3, len(loads)):
-        loads[i].wait()
-    turn(n_lat, n_lon, off, weight, off_t, w_t)
-    factor(rows, vert, inverse, ratio)
 
     for i in (2, 3):
         field_copy(i).wait_recv()
@@ -399,16 +403,19 @@
                 near[pl.ds(r * PITCH + PAD + LANES, PAD), :] = corner_in[i - 4, pl.ds(PAD + at, PAD), :]
 
     diffuse_inner(rows, near, far, c0, k2)
-    for i in (0, 1):
-        guard(-WAYS[i][0], lambda i=i: field_copy(i).wait_recv())
-        start = (STEPS + rows) if i == 0 else 0
-
-        def far_row(r, carry, i=i, start=start):
-            block = far_rows[i, aligned(r * layers, layers), :]
-            near[aligned((r + start) * PITCH + PAD, LANES), :] = upright(block)
-            return carry
-
-        lax.fori_loop(0, STEPS, far_row, 0, unroll=2)
+    for part in (0, 1):
+        for i in (0, 1):
+            guard(-WAYS[i][0], lambda i=i, part=part: field_copy(i, part).wait_recv())
+            start = (STEPS + rows) if i == 0 else 0
+
+            def far_row(r, carry, i=i, start=start):
+                block = far_rows[i, aligned(r * layers, layers), :]
+                near[aligned((r + start) * PITCH + PAD, LANES), :] = upright(block)
+                return carry
+
+            first = part * (STEPS // 2)
+            lax.fori_loop(first, first + STEPS // 2, far_row, 0, unroll=True)
+
     diffuse_rest(rows, near, far, c0, k2)
 
     def back_row(r, carry):
@@ -420,6 +427,8 @@
     for i, way in enumerate(WAYS):
         guard(way[0], lambda i=i: coef_copy(i).wait_send())
         guard(way[0], lambda i=i: field_copy(i).wait_send())
+        if way[1] == 0:
+            guard(way[0], lambda i=i: field_copy(i, 1).wait_send())
 
 
 def pick(table, row, col):
@@ -657,8 +666,8 @@
             dma((4 + 2 * blocks,)),
             dma((len(WAYS),)),
             dma((len(WAYS),)),
-            dma((len(WAYS),)),
-            dma((len(WAYS),)),
+            dma((2 * len(WAYS),)),
+            dma((2 * len(WAYS),)),
         ],
         compiler_params=pltpu.CompilerParams(
             vmem_limit_bytes=44 * 1024 * 1024, collective_id=2, has_side_effects=True

time: 36.9 us -> 35.7 us (0.967)
  Pallas kernels: 34.5 us -> 33.3 us
    pallas_call x1, Pallas kernels: 21.3 us -> 20.5 us  [per_device(): pl.pallas_call(functools.partial(field_kernel, *place, rows, layers), out...]
    pallas_call x1, Pallas kernels: 13.2 us -> 12.8 us  [per_device(): pl.pallas_call(functools.partial(observe_kernel, *place, rows, layers), o...]
where the time goes in v6:
time: 35.7 us; the launch traced here: 35.5 us
  Pallas kernels  33.3 us (93%)
  local copies, waits for them, and re-layouts  0.85 us (2%)
  between operations  0.68 us (2%)
  other arithmetic  0.62 us (2%)
    pallas_call x1, Pallas kernels, per_device(): pl.pallas_call(functools.partial(field_kernel, *place, rows, layers), out...  20.5 us
    pallas_call x1, Pallas kernels, per_device(): pl.pallas_call(functools.partial(observe_kernel, *place, rows, layers), o...  12.8 us
    unnamed x5, local copies, waits for them, and re-layouts  0.85 us

profile of v6, /device:TPU:0, one launch (start us, length us, event | category | flops | bytes accessed | tf_op | source)
XLA Modules:
  0.0 35.5 jit_solution(4200129008377646097)
XLA Ops:
  0.6 20.5 %field.1 = (f32[1280,128]{1,0:T(8,128)S(1)}, s32[2,1040,128]{2,1,0:T(8,128)S(1)}, f32[2,1040,128]{2,1,0:T(8,128)S(1)}) custom-call(f32[1280,128]{1,0:T(8,128)} %bitcast.12, f32[16,128]{1,0:T(8,128)} %kappa_ref.1, s32[16,128]{1,0:T(8,128)} %mask_ref.1, f32[320,128]{1,0:T(8,128)} %bitcast.13, s32[256,1024]{1,0:T(8,128)} %bitcast.10, f32[256,1024]{1,0:T(8,128)} %bitcast.11), custom_call_target="tpu_custom_call" | custom-call | tf_op jit(solution)/shard_map/field/pallas_call | solution.py:635
  21.2 0.0 copy-start
  21.2 0.0 copy-start.1
  21.2 12.8 %observe.1 = f32[64,128]{1,0:T(8,128)S(1)} custom-call(f32[1280,128]{1,0:T(8,128)S(1)} %get-tuple-element.5.inc_ref, s32[2,1040,128]{2,1,0:T(8,128)S(1)} %get-tuple-element.6.off_t, f32[2,1040,128]{2,1,0:T(8,128)S(1)} %get-tuple-element.7.w_t, s32[32,1024]{1,0:T(8,128)} %target_ref.1), custom_call_target="tpu_custom_call" | custom-call | tf_op jit(solution)/shard_map/observe/pallas_call | solution.py:678
  34.0 0.0 copy-done
  34.0 0.0 copy-done.1
  34.0 0.6 %fusion = f32[8192]{0:T(1024)} fusion(f32[8192]{0:T(1024)S(1)} %copy-done, f32[8192]{0:T(1024)S(1)} %copy-done.1, f32[64,128]{1,0:T(8,128)S(1)} %observe.1), kind=kLoop, calls=%fused_computation.1 | loop fusion | flops 16384 | bytes 131072 | tf_op jit(solution)/shard_map/mul | solution.py:698
  34.6 0.8 %copy.12 = f32[20,4,16,128]{3,2,1,0:T(8,128)} copy(f32[20,4,16,128]{3,2,1,0:T(8,128)S(1)} %bitcast.9) | data formatting | bytes 1310720
Async XLA Ops:
  21.2 12.8 %copy-start = (f32[8192]{0:T(1024)S(1)}, f32[8192]{0:T(1024)}, u32[]{:S(2)}) copy-start(f32[8192]{0:T(1024)} %param.17) | copy-start | bytes 98308
  21.2 12.8 %copy-start.1 = (f32[8192]{0:T(1024)S(1)}, f32[8192]{0:T(1024)}, u32[]{:S(2)}) copy-start(f32[8192]{0:T(1024)} %param.16) | copy-start | bytes 98308

commit v7 on v6

--- a/solution.py
+++ b/solution.py
@@ -60,7 +60,7 @@
 
 
 def span(old, new, c0, k2, first, count, low, high):
-    per = 5 if count % 5 == 0 else 4
+    per = 5 if count % 10 == 0 and count < 20 else 6
     update(old, new, c0, k2, count // per, first, low, high, per)
     if count % per:
         update(old, new, c0, k2, 1, first + count // per * per, low, high, count % per)
@@ -80,13 +80,10 @@
     for first in (2, STEPS + rows - 2):
         span(new, old, c0, k2, first, STEPS, 1, width - 1)
 
-    def two_steps(s, carry):
-        first = 2 * s + 1
-        update(old, new, c0, k2, (tall - 2 * first + 2) // 4, first, 1, width - 1, 4)
-        update(new, old, c0, k2, (tall - 2 * first) // 4, first + 1, 1, width - 1, 4)
-        return carry
-
-    lax.fori_loop(1, STEPS // 2, two_steps, 0)
+    for s in range(2, STEPS):
+        edge = 1 if s < STEPS - 1 else PAD // SUB
+        span(old, new, c0, k2, s + 1, tall - 2 - 2 * s, edge, width - edge)
+        old, new = new, old
 
 
 def factor(rows, vert, inverse, ratio):
@@ -490,7 +487,7 @@
         )
         return carry
 
-    lax.fori_loop(1, devices, greet, 0)
+    lax.fori_loop(1, devices, greet, 0, unroll=True)
 
     def toward(t):
         return lax.rem(mine + t + 1, passes)

time: 35.7 us -> 35.2 us (0.986)
  Pallas kernels: 33.3 us -> 32.8 us
    pallas_call x1, Pallas kernels: 20.5 us -> 20.1 us  [per_device(): pl.pallas_call(functools.partial(field_kernel, *place, rows, layers), out...]
where the time goes in v7:
time: 35.2 us; the launch traced here: 34.9 us
  Pallas kernels  32.8 us (93%)
  local copies, waits for them, and re-layouts  0.85 us (2%)
  between operations  0.68 us (2%)
  other arithmetic  0.62 us (2%)
    pallas_call x1, Pallas kernels, per_device(): pl.pallas_call(functools.partial(field_kernel, *place, rows, layers), out...  20.1 us
    pallas_call x1, Pallas kernels, per_device(): pl.pallas_call(functools.partial(observe_kernel, *place, rows, layers), o...  12.6 us
    unnamed x5, local copies, waits for them, and re-layouts  0.85 us

profile of v7, /device:TPU:0, one launch (start us, length us, event | category | flops | bytes accessed | tf_op | source)
XLA Modules:
  0.0 34.9 jit_solution(10752450286435284079)
XLA Ops:
  0.6 20.1 %field.1 = (f32[1280,128]{1,0:T(8,128)S(1)}, s32[2,1040,128]{2,1,0:T(8,128)S(1)}, f32[2,1040,128]{2,1,0:T(8,128)S(1)}) custom-call(f32[1280,128]{1,0:T(8,128)} %bitcast.12, f32[16,128]{1,0:T(8,128)} %kappa_ref.1, s32[16,128]{1,0:T(8,128)} %mask_ref.1, f32[320,128]{1,0:T(8,128)} %bitcast.13, s32[256,1024]{1,0:T(8,128)} %bitcast.10, f32[256,1024]{1,0:T(8,128)} %bitcast.11), custom_call_target="tpu_custom_call" | custom-call | tf_op jit(solution)/shard_map/field/pallas_call | solution.py:632
  20.8 0.0 copy-start
  20.8 0.0 copy-start.1
  20.8 12.6 %observe.1 = f32[64,128]{1,0:T(8,128)S(1)} custom-call(f32[1280,128]{1,0:T(8,128)S(1)} %get-tuple-element.5.inc_ref, s32[2,1040,128]{2,1,0:T(8,128)S(1)} %get-tuple-element.6.off_t, f32[2,1040,128]{2,1,0:T(8,128)S(1)} %get-tuple-element.7.w_t, s32[32,1024]{1,0:T(8,128)} %target_ref.1), custom_call_target="tpu_custom_call" | custom-call | tf_op jit(solution)/shard_map/observe/pallas_call | solution.py:675
  33.5 0.0 copy-done
  33.5 0.0 copy-done.1
  33.5 0.6 %fusion = f32[8192]{0:T(1024)} fusion(f32[8192]{0:T(1024)S(1)} %copy-done, f32[8192]{0:T(1024)S(1)} %copy-done.1, f32[64,128]{1,0:T(8,128)S(1)} %observe.1), kind=kLoop, calls=%fused_computation.1 | loop fusion | flops 16384 | bytes 131072 | tf_op jit(solution)/shard_map/mul | solution.py:695
  34.1 0.8 %copy.12 = f32[20,4,16,128]{3,2,1,0:T(8,128)} copy(f32[20,4,16,128]{3,2,1,0:T(8,128)S(1)} %bitcast.9) | data formatting | bytes 1310720
Async XLA Ops:
  20.8 12.7 %copy-start = (f32[8192]{0:T(1024)S(1)}, f32[8192]{0:T(1024)}, u32[]{:S(2)}) copy-start(f32[8192]{0:T(1024)} %param.17) | copy-start | bytes 98308
  20.8 12.7 %copy-start.1 = (f32[8192]{0:T(1024)S(1)}, f32[8192]{0:T(1024)}, u32[]{:S(2)}) copy-start(f32[8192]{0:T(1024)} %param.16) | copy-start | bytes 98308

commit v8 on v7

--- a/solution.py
+++ b/solution.py
@@ -12,7 +12,7 @@
 SUB = 8
 
 
-GROUP = 8
+GROUP = 16
 WAYS = ((-1, 0), (1, 0), (0, -1), (0, 1), (-1, -1), (-1, 1), (1, -1), (1, 1))
 PAD = 16
 PITCH = LANES + 2 * PAD
@@ -345,7 +345,7 @@
         near[aligned((r + STEPS) * PITCH + PAD, LANES), :] = upright(block)
         return carry
 
-    lax.fori_loop(0, rows, main_row, 0, unroll=2)
+    lax.fori_loop(0, rows, main_row, 0, unroll=8)
     for k, first in ((0, PAD), (1, PAD + LANES - STEPS)):
         for r in range(rows):
             side_out[k, pl.ds(r * STEPS, PAD), :] = near[
@@ -419,7 +419,7 @@
         done[aligned(r * LANES, LANES), :] = near[aligned((r + STEPS) * PITCH + PAD, LANES), :].T
         return carry
 
-    lax.fori_loop(0, rows, back_row, 0, unroll=2)
+    lax.fori_loop(0, rows, back_row, 0, unroll=8)
     solve_columns(rows, layers, done, control, coefs.at[1], vert, inverse, ratio, inc_ref)
     for i, way in enumerate(WAYS):
         guard(way[0], lambda i=i: coef_copy(i).wait_send())

time: 35.2 us -> 34.4 us (0.977)
  Pallas kernels: 32.8 us -> 32 us
    pallas_call x1, Pallas kernels: 20.1 us -> 19.3 us  [per_device(): pl.pallas_call(functools.partial(field_kernel, *place, rows, layers), out...]
where the time goes in v8:
time: 34.4 us; the launch traced here: 34.1 us
  Pallas kernels  32 us (93%)
  local copies, waits for them, and re-layouts  0.85 us (2%)
  between operations  0.68 us (2%)
  other arithmetic  0.62 us (2%)
    pallas_call x1, Pallas kernels, per_device(): pl.pallas_call(functools.partial(field_kernel, *place, rows, layers), out...  19.3 us
    pallas_call x1, Pallas kernels, per_device(): pl.pallas_call(functools.partial(observe_kernel, *place, rows, layers), o...  12.7 us
    unnamed x5, local copies, waits for them, and re-layouts  0.85 us

profile of v8, /device:TPU:0, one launch (start us, length us, event | category | flops | bytes accessed | tf_op | source)
XLA Modules:
  0.0 34.1 jit_solution(5219093026777824969)
XLA Ops:
  0.6 19.3 %field.1 = (f32[1280,128]{1,0:T(8,128)S(1)}, s32[2,1040,128]{2,1,0:T(8,128)S(1)}, f32[2,1040,128]{2,1,0:T(8,128)S(1)}) custom-call(f32[1280,128]{1,0:T(8,128)} %bitcast.12, f32[16,128]{1,0:T(8,128)} %kappa_ref.1, s32[16,128]{1,0:T(8,128)} %mask_ref.1, f32[320,128]{1,0:T(8,128)} %bitcast.13, s32[256,1024]{1,0:T(8,128)} %bitcast.10, f32[256,1024]{1,0:T(8,128)} %bitcast.11), custom_call_target="tpu_custom_call" | custom-call | tf_op jit(solution)/shard_map/field/pallas_call | solution.py:632
  20.0 0.0 copy-start
  20.0 0.0 copy-start.1
  20.0 12.7 %observe.1 = f32[64,128]{1,0:T(8,128)S(1)} custom-call(f32[1280,128]{1,0:T(8,128)S(1)} %get-tuple-element.5.inc_ref, s32[2,1040,128]{2,1,0:T(8,128)S(1)} %get-tuple-element.6.off_t, f32[2,1040,128]{2,1,0:T(8,128)S(1)} %get-tuple-element.7.w_t, s32[32,1024]{1,0:T(8,128)} %target_ref.1), custom_call_target="tpu_custom_call" | custom-call | tf_op jit(solution)/shard_map/observe/pallas_call | solution.py:675
  32.7 0.0 copy-done
  32.7 0.0 copy-done.1
  32.7 0.6 %fusion = f32[8192]{0:T(1024)} fusion(f32[8192]{0:T(1024)S(1)} %copy-done, f32[8192]{0:T(1024)S(1)} %copy-done.1, f32[64,128]{1,0:T(8,128)S(1)} %observe.1), kind=kLoop, calls=%fused_computation.1 | loop fusion | flops 16384 | bytes 131072 | tf_op jit(solution)/shard_map/mul | solution.py:695
  33.3 0.8 %copy.12 = f32[20,4,16,128]{3,2,1,0:T(8,128)} copy(f32[20,4,16,128]{3,2,1,0:T(8,128)S(1)} %bitcast.9) | data formatting | bytes 1310720
Async XLA Ops:
  20.0 12.7 %copy-start = (f32[8192]{0:T(1024)S(1)}, f32[8192]{0:T(1024)}, u32[]{:S(2)}) copy-start(f32[8192]{0:T(1024)} %param.17) | copy-start | bytes 98308
  20.0 12.7 %copy-start.1 = (f32[8192]{0:T(1024)S(1)}, f32[8192]{0:T(1024)}, u32[]{:S(2)}) copy-start(f32[8192]{0:T(1024)} %param.16) | copy-start | bytes 98308

commit v9 on v8

--- a/solution.py
+++ b/solution.py
@@ -260,7 +260,7 @@
         here = pl.ds(c * LANES, LANES)
         pairs += ((off_ref.at[:, here], off.at[c]), (w_ref.at[:, here], weight.at[c]))
     loads = [pltpu.make_async_copy(a, b, load_sem.at[i]) for i, (a, b) in enumerate(pairs)]
-    for i in (1, 2, 0, *range(3, len(loads))):
+    for i in (1, 2, 0):
         loads[i].start()
 
     def place(i):
@@ -327,6 +327,8 @@
             src, dst = corner_sent.at[i - 4], corner_got.at[i - 4]
         return remote(i, src, dst, send_sem, recv_sem, part)
 
+    for i in range(3, len(loads)):
+        loads[i].start()
     loads[1].wait()
     loads[2].wait()
     coefs[1, pl.ds(rows, rows), :] = kappa[...] * mask[...].astype(jnp.float32)
@@ -345,7 +347,7 @@
         near[aligned((r + STEPS) * PITCH + PAD, LANES), :] = upright(block)
         return carry
 
-    lax.fori_loop(0, rows, main_row, 0, unroll=8)
+    lax.fori_loop(0, rows, main_row, 0, unroll=True)
     for k, first in ((0, PAD), (1, PAD + LANES - STEPS)):
         for r in range(rows):
             side_out[k, pl.ds(r * STEPS, PAD), :] = near[
@@ -363,7 +365,7 @@
     pl.semaphore_wait(barrier, 2 + 3 * beside)
     for i, way in enumerate(WAYS):
         guard(way[0], lambda i=i: coef_copy(i).start())
-    for i in (2, 3, 0, 1, 4, 5, 6, 7):
+    for i in (2, 3, 4, 5, 6, 7, 0, 1):
         guard(WAYS[i][0], lambda i=i: field_copy(i).start())
     for i in (0, 1):
         guard(WAYS[i][0], lambda i=i: field_copy(i, 1).start())
@@ -419,7 +421,7 @@
         done[aligned(r * LANES, LANES), :] = near[aligned((r + STEPS) * PITCH + PAD, LANES), :].T
         return carry
 
-    lax.fori_loop(0, rows, back_row, 0, unroll=8)
+    lax.fori_loop(0, rows, back_row, 0, unroll=True)
     solve_columns(rows, layers, done, control, coefs.at[1], vert, inverse, ratio, inc_ref)
     for i, way in enumerate(WAYS):
         guard(way[0], lambda i=i: coef_copy(i).wait_send())

time: 34.4 us -> 34.1 us (level)
    pallas_call x1, Pallas kernels: 19.3 us -> 18.9 us  [per_device(): pl.pallas_call(functools.partial(field_kernel, *place, rows, layers), out...]
where the time goes in v9:
time: 34.1 us; the launch traced here: 33.9 us
  Pallas kernels  31.7 us (93%)
  local copies, waits for them, and re-layouts  0.85 us (2%)
  between operations  0.68 us (2%)
  other arithmetic  0.62 us (2%)
    pallas_call x1, Pallas kernels, per_device(): pl.pallas_call(functools.partial(field_kernel, *place, rows, layers), out...  18.9 us
    pallas_call x1, Pallas kernels, per_device(): pl.pallas_call(functools.partial(observe_kernel, *place, rows, layers), o...  12.8 us
    unnamed x5, local copies, waits for them, and re-layouts  0.85 us

profile of v9, /device:TPU:0, one launch (start us, length us, event | category | flops | bytes accessed | tf_op | source)
XLA Modules:
  0.0 33.9 jit_solution(4849491684893873600)
XLA Ops:
  0.6 18.9 %field.1 = (f32[1280,128]{1,0:T(8,128)S(1)}, s32[2,1040,128]{2,1,0:T(8,128)S(1)}, f32[2,1040,128]{2,1,0:T(8,128)S(1)}) custom-call(f32[1280,128]{1,0:T(8,128)} %bitcast.12, f32[16,128]{1,0:T(8,128)} %kappa_ref.1, s32[16,128]{1,0:T(8,128)} %mask_ref.1, f32[320,128]{1,0:T(8,128)} %bitcast.13, s32[256,1024]{1,0:T(8,128)} %bitcast.10, f32[256,1024]{1,0:T(8,128)} %bitcast.11), custom_call_target="tpu_custom_call" | custom-call | tf_op jit(solution)/shard_map/field/pallas_call | solution.py:634
  19.6 0.0 copy-start
  19.6 0.0 copy-start.1
  19.6 12.8 %observe.1 = f32[64,128]{1,0:T(8,128)S(1)} custom-call(f32[1280,128]{1,0:T(8,128)S(1)} %get-tuple-element.5.inc_ref, s32[2,1040,128]{2,1,0:T(8,128)S(1)} %get-tuple-element.6.off_t, f32[2,1040,128]{2,1,0:T(8,128)S(1)} %get-tuple-element.7.w_t, s32[32,1024]{1,0:T(8,128)} %target_ref.1), custom_call_target="tpu_custom_call" | custom-call | tf_op jit(solution)/shard_map/observe/pallas_call | solution.py:677
  32.4 0.0 copy-done
  32.4 0.0 copy-done.1
  32.4 0.6 %fusion = f32[8192]{0:T(1024)} fusion(f32[8192]{0:T(1024)S(1)} %copy-done, f32[8192]{0:T(1024)S(1)} %copy-done.1, f32[64,128]{1,0:T(8,128)S(1)} %observe.1), kind=kLoop, calls=%fused_computation.1 | loop fusion | flops 16384 | bytes 131072 | tf_op jit(solution)/shard_map/mul | solution.py:697
  33.0 0.8 %copy.12 = f32[20,4,16,128]{3,2,1,0:T(8,128)} copy(f32[20,4,16,128]{3,2,1,0:T(8,128)S(1)} %bitcast.9) | data formatting | bytes 1310720
Async XLA Ops:
  19.6 12.8 %copy-start = (f32[8192]{0:T(1024)S(1)}, f32[8192]{0:T(1024)}, u32[]{:S(2)}) copy-start(f32[8192]{0:T(1024)} %param.17) | copy-start | bytes 98308
  19.6 12.8 %copy-start.1 = (f32[8192]{0:T(1024)S(1)}, f32[8192]{0:T(1024)}, u32[]{:S(2)}) copy-start(f32[8192]{0:T(1024)} %param.16) | copy-start | bytes 98308
